TPU v7x, 32 devices: a whole 2x2x4 slice. The times are simulated.
32 devices in a mesh: img: 2 (over x), tile: 16 (over z, y, core).
Axes of the slice: x: 2, y: 2, z: 4, core: 2. Of those that a mesh axis runs over, the one named last changes fastest.
Arguments:
- block_feature_map: bfloat16 [2, 192, 128, 256], P('img', None, 'tile'), may hold values from -12 to 12, as said below
- upstream_sensitivity: bfloat16 [2, 192, 128, 256], P('img', None, 'tile'), may hold values from -12 to 12, as said below
- triple_mixer: bfloat16 [576, 192], replicated, may hold values from -0.4375 to 0.4375
- spatial_stencil: float32 [576, 3, 3], replicated, may hold values from -2 to 2
- outgoing_mixer: bfloat16 [192, 192], replicated, may hold values from -0.4375 to 0.4375
- sharpness_factor: float32 [4], replicated, may hold values from 1 to 8
- standardize_scaling: float32 [192], replicated, may hold values from 0.5 to 1.5
- standardize_offset: float32 [192], replicated, may hold values from -1.5 to 1.5
Outputs:
- feature_map_adjoint: bfloat16 [2, 192, 128, 256], P('img', None, 'tile')
- triple_mixer_adjoint: float32 [576, 192], replicated
- spatial_stencil_adjoint: float32 [576, 3, 3], replicated
- outgoing_mixer_adjoint: float32 [192, 192], replicated
- sharpness_adjoint: float32 [4], replicated
- scaling_adjoint: float32 [192], replicated
- offset_adjoint: float32 [192], replicated
Inputs may be any that keep to these rules, and one draw needn't show every extreme that they name: `block_feature_map`: the block's input feature map. `upstream_sensitivity`: gradient of the loss with respect to the block's output.
All inputs are finite; a program needn't handle non-finite values.
Results may differ from a plain program's by a relative error of at most 0.0072.
Values may be sent and summed in bfloat16 or wider, within the bound.
A program may use at most 64 MiB of HBM per device.

v0:
```python
import jax
import jax.numpy as jnp
from jax import lax
from jax.sharding import PartitionSpec as P


def padded_2(array, sides, width):
    for axis, dim in sides:
        count, length = (lax.axis_size(axis), array.shape[dim])
        up = [(i, (i + 1) % count) for i in range(count - 1)]
        down = [(j, i) for i, j in up]
        last = lax.slice_in_dim(array, length - width, length, axis=dim)
        leading = lax.slice_in_dim(array, 0, width, axis=dim)
        before = lax.ppermute(last, axis, up)
        after = lax.ppermute(leading, axis, down)
        array = jnp.concatenate([before, array, after], axis=dim)
    return array


def depthwise(padded, spatial_stencil):
    row_count = padded.shape[-2] - 2
    col_count = padded.shape[-1]
    widened = jnp.pad(padded.astype(jnp.float32), [(0, 0)] * (padded.ndim - 1) + [(1, 1)])
    summed = jnp.zeros(padded.shape[:-2] + (row_count, col_count), jnp.float32)
    for row_off in range(3):
        for col_off in range(3):
            summed = (
                summed
                + spatial_stencil[:, row_off, col_off, None, None]
                * widened[..., row_off : row_off + row_count, col_off : col_off + col_count]
            )
    return summed


def depthwise_back(padded, spatial_stencil):
    row_count = padded.shape[-2] - 2
    col_count = padded.shape[-1]
    widened = jnp.pad(padded.astype(jnp.float32), [(0, 0)] * (padded.ndim - 1) + [(1, 1)])
    summed = jnp.zeros(padded.shape[:-2] + (row_count, col_count), jnp.float32)
    for row_off in range(3):
        for col_off in range(3):
            summed = (
                summed
                + spatial_stencil[:, row_off, col_off, None, None]
                * widened[
                    ...,
                    2 - row_off : 2 - row_off + row_count,
                    2 - col_off : 2 - col_off + col_count,
                ]
            )
    return summed


def kernel_grad(grad_mixed, padded):
    row_count = grad_mixed.shape[-2]
    col_count = grad_mixed.shape[-1]
    grad_float = grad_mixed.astype(jnp.float32)
    widened = jnp.pad(padded.astype(jnp.float32), [(0, 0)] * (padded.ndim - 1) + [(1, 1)])
    reduce_axes = tuple((i for i in range(grad_mixed.ndim) if i != grad_mixed.ndim - 3))
    partials = []
    for row_off in range(3):
        for col_off in range(3):
            partials.append(
                jnp.sum(
                    grad_float
                    * widened[..., row_off : row_off + row_count, col_off : col_off + col_count],
                    axis=reduce_axes,
                )
            )
    return jnp.stack(partials, axis=-1).reshape(grad_mixed.shape[-3], 3, 3)


def local(
    block_feature_map,
    upstream_sensitivity,
    triple_mixer,
    spatial_stencil,
    outgoing_mixer,
    sharpness_factor,
    standardize_scaling,
    standardize_offset,
):
    images, channels, row_count, col_count = block_feature_map.shape
    group_ordinal = sharpness_factor.shape[0]
    head_size = channels // group_ordinal
    pixel_count = row_count * col_count
    as_float = block_feature_map.astype(jnp.float32)
    average = jnp.mean(as_float, axis=1, keepdims=True)
    centered = as_float - average
    inverse = lax.rsqrt(jnp.mean(centered * centered, axis=1, keepdims=True) + 1e-05)
    standard = centered * inverse
    normed = (
        standard * standardize_scaling[:, None, None] + standardize_offset[:, None, None]
    ).astype(jnp.bfloat16)
    projected = jnp.einsum(
        "oc,bchw->bohw", triple_mixer, normed, preferred_element_type=jnp.float32
    ).astype(jnp.bfloat16)
    padded = padded_2(projected, (("tile", 2),), 1)
    mixed = depthwise(padded, spatial_stencil).astype(jnp.bfloat16)
    query_part = mixed[:, :channels].reshape(images, group_ordinal, head_size, pixel_count)
    key_part = mixed[:, channels : 2 * channels].reshape(
        images, group_ordinal, head_size, pixel_count
    )
    value_part = mixed[:, 2 * channels :].reshape(images, group_ordinal, head_size, pixel_count)
    gram_raw = jnp.einsum(
        "bhip,bhjp->bhij", query_part, key_part, preferred_element_type=jnp.float32
    )
    query_float = query_part.astype(jnp.float32)
    key_float = key_part.astype(jnp.float32)
    query_sq = jnp.sum(query_float * query_float, axis=3)
    key_sq = jnp.sum(key_float * key_float, axis=3)
    flat_dy = upstream_sensitivity.reshape(images, channels, pixel_count)
    gram_raw, query_sq, key_sq = lax.psum((gram_raw, query_sq, key_sq), "tile")
    query_len = jnp.sqrt(query_sq + 1e-06)
    key_len = jnp.sqrt(key_sq + 1e-06)
    normalized_affinity = gram_raw / (query_len[..., :, None] * key_len[..., None, :])
    normalized_exp_logits = jnp.exp(normalized_affinity * sharpness_factor[None, :, None, None])
    attention = normalized_exp_logits / jnp.sum(normalized_exp_logits, axis=3, keepdims=True)
    attention_b = attention.astype(jnp.bfloat16)
    attended = jnp.einsum(
        "bhij,bhjp->bhip", attention_b, value_part, preferred_element_type=jnp.float32
    ).astype(jnp.bfloat16)
    flat_out = attended.reshape(images, channels, pixel_count)
    outgoing_mixer_adjoint = jnp.einsum(
        "bop,bcp->oc", flat_dy, flat_out, preferred_element_type=jnp.float32
    )
    grad_attended = jnp.einsum(
        "oc,bop->bcp", outgoing_mixer, flat_dy, preferred_element_type=jnp.float32
    ).astype(jnp.bfloat16)
    grad_attended = grad_attended.reshape(images, group_ordinal, head_size, pixel_count)
    grad_attention = jnp.einsum(
        "bhip,bhjp->bhij", grad_attended, value_part, preferred_element_type=jnp.float32
    )
    grad_attention = lax.psum(grad_attention, "tile")
    grad_value = jnp.einsum(
        "bhij,bhip->bhjp", attention_b, grad_attended, preferred_element_type=jnp.float32
    )
    logits_adjoint = attention * (
        grad_attention - jnp.sum(attention * grad_attention, axis=3, keepdims=True)
    )
    leading_accelerator = (lax.axis_index("tile") == 0).astype(jnp.float32)
    sharpness_adjoint = leading_accelerator * jnp.sum(
        logits_adjoint * normalized_affinity, axis=(0, 2, 3)
    )
    affinity_adjoint = logits_adjoint * sharpness_factor[None, :, None, None]
    grad_gram = (affinity_adjoint / (query_len[..., :, None] * key_len[..., None, :])).astype(
        jnp.bfloat16
    )
    grad_query = jnp.einsum(
        "bhij,bhjp->bhip", grad_gram, key_part, preferred_element_type=jnp.float32
    )
    grad_key = jnp.einsum(
        "bhij,bhip->bhjp", grad_gram, query_part, preferred_element_type=jnp.float32
    )
    product_terms = affinity_adjoint * normalized_affinity
    row_terms = jnp.sum(product_terms, axis=3)
    col_terms = jnp.sum(product_terms, axis=2)
    grad_query = grad_query - query_float * (row_terms / (query_sq + 1e-06))[..., None]
    grad_key = grad_key - key_float * (col_terms / (key_sq + 1e-06))[..., None]
    grad_mixed = jnp.concatenate([grad_query, grad_key, grad_value], axis=1)
    grad_mixed = grad_mixed.reshape(images, 3 * channels, row_count, col_count).astype(jnp.bfloat16)
    grad_padded = padded_2(grad_mixed, (("tile", 2),), 1)
    grad_projected = depthwise_back(grad_padded, spatial_stencil).astype(jnp.bfloat16)
    spatial_stencil_adjoint = kernel_grad(grad_mixed, padded)
    flat_gproj = grad_projected.reshape(images, 3 * channels, pixel_count)
    triple_mixer_adjoint = jnp.einsum(
        "bop,bcp->oc",
        flat_gproj,
        normed.reshape(images, channels, pixel_count),
        preferred_element_type=jnp.float32,
    )
    grad_normed = jnp.einsum(
        "oc,bop->bcp", triple_mixer, flat_gproj, preferred_element_type=jnp.float32
    )
    grad_normed = grad_normed.reshape(images, channels, row_count, col_count)
    scaling_adjoint = jnp.sum(grad_normed * standard, axis=(0, 2, 3))
    offset_adjoint = jnp.sum(grad_normed, axis=(0, 2, 3))
    scaled = grad_normed * standardize_scaling[:, None, None]
    first_mean = jnp.mean(scaled, axis=1, keepdims=True)
    second_mean = jnp.mean(scaled * standard, axis=1, keepdims=True)
    feature_map_adjoint = (
        upstream_sensitivity.astype(jnp.float32)
        + (scaled - first_mean - standard * second_mean) * inverse
    ).astype(jnp.bfloat16)
    (
        triple_mixer_adjoint,
        spatial_stencil_adjoint,
        outgoing_mixer_adjoint,
        sharpness_adjoint,
        scaling_adjoint,
        offset_adjoint,
    ) = lax.psum(
        (
            triple_mixer_adjoint,
            spatial_stencil_adjoint,
            outgoing_mixer_adjoint,
            sharpness_adjoint,
            scaling_adjoint,
            offset_adjoint,
        ),
        ("img", "tile"),
    )
    return (
        feature_map_adjoint,
        triple_mixer_adjoint,
        spatial_stencil_adjoint,
        outgoing_mixer_adjoint,
        sharpness_adjoint,
        scaling_adjoint,
        offset_adjoint,
    )


def solution(mesh):
    return jax.shard_map(
        local,
        mesh=mesh,
        in_specs=(
            P("img", None, "tile", None),
            P("img", None, "tile", None),
            P(),
            P(),
            P(),
            P(),
            P(),
            P(),
        ),
        out_specs=(P("img", None, "tile", None), P(), P(), P(), P(), P(), P()),
        check_vma=False,
    )
```

profile of v0, /device:TPU:0, one launch (start us, length us, event | category | flops | bytes accessed | tf_op | source)
XLA Modules:
  0.0 355.5 jit_solution(12298602474802299675)
XLA Ops:
  7.3 1.4 convert_reduce_fusion
  8.7 1.4 fusion.42
  10.1 1.6 fusion.47
  12.6 2.4 collective-permute-start
  15.0 1.3 collective-permute-start.1
  17.1 3.5 collective-permute-done.1
  21.1 8.7 %add_convert_fusion = bf16[1,576,8,256]{3,1,2,0:T(8,128)(2,1)S(1)} fusion(f32[1,576,10,256]{3,1,2,0:T(8,128)S(1)} %maximum_convert_fusion.1, f32[576]{0:T(1024)S(1)} %get-tuple-element.44, f32[576]{0:T(1024)S(1)} %get-tuple-element.45, f32[576]{0:T(1024)S(1)} %get-tuple-element.38, f32[576]{0:T(1024)S(1)} %get-tuple-element.39, ...), kind=kLoop, calls=%fused_computation.49 | loop fusion | flops 21233664 | bytes 22450176 | tf_op jit(solution)/shard_map/convert_element_type | solution.py:99
  30.4 1.3 copy.23
  31.7 2.2 reshape.358
  35.2 1.3 copy.22
  36.6 1.4 reshape.355
  38.0 1.3 copy.21
  39.3 1.4 reshape.354
  40.8 2.1 convolution_bitcast_fusion.2
  44.2 93.8 %all-reduce.10.cloned.1.call-done = (f32[1,4,48,48]{3,2,1,0:T(8,128)}, f32[1,4,48]{2,1,0:T(4,128)}, f32[1,4,48]{2,1,0:T(4,128)}, f32[1,4,48,48]{3,2,1,0:T(8,128)}) async-done(((f32[1,4,48,48]{3,2,1,0:T(8,128)}, f32[1,4,48]{2,1,0:T(4,128)}, f32[1,4,48]{2,1,0:T(4,128)}, f32[1,4,48,48]{3,2,1,0:T(8,128)}), (f32[1,4,48,48]{3,2,1,0:T(8,128)}, f32[1,4,48]{2,1,0:T(4,128)}, f32[1,4,48]{2,1,0:T(4,128)}, ...) | async-done | bytes 75280 | tf_op jit(solution)/shard_map/psum | solution.py:113
  139.8 1.4 convolution_bitcast_fusion
  141.2 2.5 convolution_convert_fusion
  150.8 12.1 %fusion.23 = (f32[576]{0:T(1024)S(1)}, f32[576]{0:T(1024)S(1)}, f32[576]{0:T(1024)S(1)}, f32[576]{0:T(1024)S(1)}, f32[576]{0:T(1024)S(1)}, /*index=5*/f32[576]{0...) fusion(f32[1,576,10,256]{3,1,2,0:T(8,128)S(1)} %bitcast.114, bf16[1,576,8,256]{3,2,1,0:T(8,128)(2,1)S(1)} %bitcast.115), kind=kLoop, calls=%fused_computation.44 | loop fusion | flops 22408128 | bytes 22434048 | tf_op jit(solution)/shard_map/reduce_sum | solution.py:64
  164.3 2.7 collective-permute-start.2
  167.0 1.5 collective-permute-start.3
  168.7 2.2 convolution_bitcast_fusion.1
  170.9 1.6 maximum_convert_fusion.2
  172.5 2.5 copy-done.2
  175.0 9.7 %fusion.44 = f32[576,192]{0,1:T(8,128)} fusion(bf16[192,8,256]{2,1,0:T(8,128)(2,1)S(1)} %copy-done.8, f32[1,576,10,256]{3,1,2,0:T(8,128)S(1)} %maximum_convert_fusion.2, f32[576]{0:T(1024)S(1)} %get-tuple-element.44, f32[576]{0:T(1024)S(1)} %get-tuple-element.45, f32[576]{0:T(1024)S(1)} %get-tuple-element.38, f32[576]{0:T(1024)S(1)} %get-tuple-element.39, ...), kind=kOutput, calls=%fused_computation.84 | convolution fusion | flops 474218496 | bytes 21319680 | tf_op jit(solution)/shard_map/bop,bcp->oc/dot_general | solution.py:166
  184.7 18.9 %fusion.85 = bf16[72,8,8,256]{3,1,0,2:T(8,128)(2,1)S(1)} fusion(f32[576]{0:T(1024)S(1)} %get-tuple-element.44, f32[1,576,10,256]{3,1,2,0:T(8,128)} %copy-done.2, f32[576]{0:T(1024)S(1)} %get-tuple-element.45, f32[576]{0:T(1024)S(1)} %get-tuple-element.38, f32[576]{0:T(1024)S(1)} %get-tuple-element.39, f32[576]{0:T(1024)S(1)} %get-tuple-element.40, ...), kind=kLoop, calls=%fused_computation.133 | loop fusion | flops 21233664 | bytes 22434048
  206.3 2.0 copy.38
  208.4 1.6 fusion.41
  210.0 48.1 %all-reduce.2 = (f32[576,3,3]{0,2,1:T(4,128)}, f32[4]{0:T(128)}, f32[192]{0:T(256)}, f32[192]{0:T(256)}) all-reduce(f32[576,3,3]{0,2,1:T(4,128)S(1)} %reshape.364, f32[4]{0:T(128)S(1)} %broadcast_multiply_fusion.3, f32[192]{0:T(256)S(1)} %get-tuple-element.30, f32[192]{0:T(256)S(1)} %reduce_sum.231), channel_id=1, replica_groups=mesh['img'=2,'tile'=16] {'img','tile'}, use_global_device_ids=true, to_apply=%region_24.25 | all-reduce | flops 5572 | bytes 44576 | tf_op jit(solution)/shard_map/psum | solution.py:192
  258.1 1.4 fusion.40
  259.5 85.6 %all-reduce.8.cloned.1.call-done = (f32[576,192]{0,1:T(8,128)}, f32[192,192]{0,1:T(8,128)}) async-done(((f32[576,192]{0,1:T(8,128)}, f32[192,192]{0,1:T(8,128)}), (f32[576,192]{0,1:T(8,128)}, f32[192,192]{0,1:T(8,128)})) %all-reduce.8.cloned.1.call-update) | async-done | bytes 589840 | tf_op jit(solution)/shard_map/psum | solution.py:192
  345.1 1.7 copy.32
  346.9 1.8 copy.59
  (80 shorter events, 18.2 us)
Async XLA Ops:
  7.2 4.6 %copy-start = (bf16[576,192]{0,1:T(8,128)(2,1)S(1)}, bf16[576,192]{0,1:T(8,128)(2,1)}, u32[]{:S(2)}) copy-start(bf16[576,192]{0,1:T(8,128)(2,1)} %param.10) | copy-start | bytes 663556
  7.2 9.1 %copy-start.11 = (f32[576,3,3]{0,2,1:T(4,128)S(1)}, f32[576,3,3]{0,2,1:T(4,128)}, u32[]{:S(2)}) copy-start(f32[576,3,3]{0,2,1:T(4,128)} %param.11) | copy-start | bytes 62212
  7.2 9.2 %copy-start.5 = (bf16[1,192,8,256]{3,2,1,0:T(8,128)(2,1)S(1)}, bf16[1,192,8,256]{3,2,1,0:T(8,128)(2,1)}, u32[]{:S(2)}) copy-start(bf16[1,192,8,256]{3,2,1,0:T(8,128)(2,1)} %param.9) | copy-start | bytes 2359300
  7.2 9.4 %copy-start.9 = (bf16[192,192]{1,0:T(8,128)(2,1)S(1)}, bf16[192,192]{1,0:T(8,128)(2,1)}, u32[]{:S(2)}) copy-start(bf16[192,192]{1,0:T(8,128)(2,1)} %param.12) | copy-start | bytes 221188
  7.2 130.8 %all-reduce.10.cloned.1.call-start = ((), (), s32[]{:S(2)}) async-start(), calls=%async_computation.1 | async-start | bytes 401408 | tf_op jit(solution)/shard_map/psum | solution.py:113
  11.8 4.7 %copy-start.7 = (bf16[192,8,256]{2,1,0:T(8,128)(2,1)}, bf16[192,8,256]{2,1,0:T(8,128)(2,1)S(1)}, u32[]{:S(2)}) copy-start(bf16[192,8,256]{2,1,0:T(8,128)(2,1)S(1)} %fusion.47) | copy-start | bytes 2359300
  12.6 4.4 %collective-permute-start = (bf16[1,576,1,256]{3,1,2,0:T(8,128)(2,1)S(1)}, bf16[1,576,1,256]{3,1,2,0:T(8,128)(2,1)S(1)}, u32[]{:S(2)}, u32[]{:S(2)}) collective-permute-start(bf16[1,576,1,256]{3,1,2,0:T(8,128)(2,1)S(1)} %get-tuple-element.62), channel_id=1, source_target_pairs={{0,1},{1,2},{2,3},{3,4},{4,5},{5,6},{6,7},{7,8},{8,9},{9,10},{10,1... | collective-permute-start | bytes 884744 | tf_op jit(solution)/shard_map/ppermute | solution.py:14
  15.0 5.6 %collective-permute-start.1 = (bf16[1,576,1,256]{3,1,2,0:T(8,128)(2,1)S(1)}, bf16[1,576,1,256]{3,1,2,0:T(8,128)(2,1)S(1)}, u32[]{:S(2)}, u32[]{:S(2)}) collective-permute-start(bf16[1,576,1,256]{3,1,2,0:T(8,128)(2,1)S(1)} %get-tuple-element.63), channel_id=1, source_target_pairs={{1,0},{2,1},{3,2},{4,3},{5,4},{6,5},{7,6},{8,7},{9,8},{10,9},{11,1... | collective-permute-start | bytes 884744 | tf_op jit(solution)/shard_map/ppermute | solution.py:15
  21.1 8.7 %copy-start.1 = (f32[1,576,10,256]{3,1,2,0:T(8,128)}, f32[1,576,10,256]{3,1,2,0:T(8,128)S(1)}, u32[]{:S(2)}) copy-start(f32[1,576,10,256]{3,1,2,0:T(8,128)S(1)} %maximum_convert_fusion.1) | copy-start | bytes 17694724
  35.2 103.4 %copy-start.10 = (f32[4]{0:T(128)S(1)}, f32[4]{0:T(128)}, u32[]{:S(2)}) copy-start(f32[4]{0:T(128)} %param.13) | copy-start | bytes 52
  43.9 301.2 %all-reduce.8.cloned.1.call-start = ((), (), s32[]{:S(2)}) async-start(), calls=%async_computation | async-start | bytes 1376256 | tf_op jit(solution)/shard_map/psum | solution.py:192
  148.0 2.2 slice-start
  148.5 2.4 slice-start.1
  164.3 6.6 %collective-permute-start.2 = (bf16[1,576,1,256]{3,1,2,0:T(8,128)(2,1)}, bf16[1,576,1,256]{3,1,2,0:T(8,128)(2,1)}, u32[]{:S(2)}, u32[]{:S(2)}) collective-permute-start(bf16[1,576,1,256]{3,1,2,0:T(8,128)(2,1)} %get-tuple-element.57), channel_id=1, source_target_pairs={{0,1},{1,2},{2,3},{3,4},{4,5},{5,6},{6,7},{7,8},{8,9},{9,10},{10,1... | collective-permute-start | bytes 884744 | tf_op jit(solution)/shard_map/ppermute | solution.py:14
  167.0 3.9 %collective-permute-start.3 = (bf16[1,576,1,256]{3,1,2,0:T(8,128)(2,1)}, bf16[1,576,1,256]{3,1,2,0:T(8,128)(2,1)}, u32[]{:S(2)}, u32[]{:S(2)}) collective-permute-start(bf16[1,576,1,256]{3,1,2,0:T(8,128)(2,1)} %get-tuple-element.58), channel_id=1, source_target_pairs={{1,0},{2,1},{3,2},{4,3},{5,4},{6,5},{7,6},{8,7},{9,8},{10,9},{11,1... | collective-permute-start | bytes 884744 | tf_op jit(solution)/shard_map/ppermute | solution.py:15
  170.9 4.1 %copy-start.8 = (bf16[192,8,256]{2,1,0:T(8,128)(2,1)S(1)}, bf16[192,8,256]{2,1,0:T(8,128)(2,1)}, u32[]{:S(2)}) copy-start(bf16[192,8,256]{2,1,0:T(8,128)(2,1)} %copy-done.7) | copy-start | bytes 2359300
  172.5 2.5 copy-start.2
  203.7 0.7 copy-start.12
  204.0 4.3 %copy-start.3 = (bf16[1,192,8,256]{3,2,1,0:T(8,128)(2,1)S(1)}, bf16[1,192,8,256]{3,2,1,0:T(8,128)(2,1)}, u32[]{:S(2)}) copy-start(bf16[1,192,8,256]{3,2,1,0:T(8,128)(2,1)} %param.8) | copy-start | bytes 2359300
  205.2 1.2 copy-start.4
  205.2 52.9 %copy-start.6 = (bf16[1,192,8,256]{3,2,1,0:T(8,128)(2,1)S(1)}, bf16[1,192,8,256]{3,2,1,0:T(8,128)(2,1)}, u32[]{:S(2)}) copy-start(bf16[1,192,8,256]{3,2,1,0:T(8,128)(2,1)} %param.9) | copy-start | bytes 2359300
Sparse Core Ops, SparseCore 0:
  44.1 93.9 all-reduce.9
  210.1 134.9 all-reduce.7
where the time goes:
time: 357 us; the launch traced here: 356 us
  waiting for transfers between devices  183 us (51%)
  other arithmetic  55.6 us (16%)
  blocking collectives  48.1 us (13%)
  local copies, waits for them, and re-layouts  24.2 us (7%)
  matrix products  22 us (6%)
  between operations  14.6 us (4%)
  starting transfers between devices  8.13 us (2%)
    psum x1, waiting for transfers between devices, local(): gram_raw, query_sq, key_sq = lax.psum((gram_raw, query_sq, key_sq), 'tile')  93.8 us
    psum x1, waiting for transfers between devices, local(): lax.psum((triple_mixer_adjoint, spatial_stencil_adjoint, outgoing_mixer_a...  85.6 us
    psum x1, blocking collectives, local(): lax.psum((triple_mixer_adjoint, spatial_stencil_adjoint, outgoing_mixer_a...  48.1 us
    unnamed x2, other arithmetic  18.9 us
    reduce_sum x1, other arithmetic, kernel_grad(): jnp.sum(grad_float * widened[..., row_off:row_off + row_count, col_off:co...  12.1 us
    unnamed x36, local copies, waits for them, and re-layouts  12 us
    dot_general x1, matrix products, local(): jnp.einsum('bop,bcp->oc', flat_gproj, normed.reshape(images, channels, pi...  9.72 us
    convert_element_type x1, other arithmetic, local(): mixed = depthwise(padded, spatial_stencil).astype(jnp.bfloat16)  8.67 us
  transfers between devices with their start and end apart: 6, of which 3 were waited for; matrix products, arithmetic and copies ran while one was open for 1% of the time, Pallas kernels for 0%

commit v1 on v0

v1 whole, which is shorter than its diff:
```python
import functools
import jax
import jax.numpy as jnp
from jax import lax
from jax.experimental import pallas as pl
from jax.experimental.pallas import tpu as pltpu
from jax.sharding import PartitionSpec as P

F32 = jnp.float32
BF16 = jnp.bfloat16
NT = (((1,), (1,)), ((), ()))
NN = (((1,), (0,)), ((), ()))
TN = (((0,), (0,)), ((), ()))
VMEM = pl.BlockSpec(memory_space=pltpu.VMEM)
SMEM = pl.BlockSpec(memory_space=pltpu.SMEM)
LIMIT = 56 * 1024 * 1024


def dot(a, b, dims=NN):
    return lax.dot_general(a, b, dims, preferred_element_type=F32)


def standardized(x):
    xf = x.astype(F32)
    centered = xf - jnp.mean(xf, axis=0, keepdims=True)
    inverse = lax.rsqrt(jnp.mean(centered * centered, axis=0, keepdims=True) + 1e-05)
    return centered * inverse, inverse


def shifted(v, lanes):
    width = v.shape[-1]
    right = jnp.where(lanes == 0, 0.0, pltpu.roll(v, 1, 1))
    left = jnp.where(lanes == width - 1, 0.0, pltpu.roll(v, width - 1, 1))
    return right, left


def forward_kernel(
    lo_ref, own_ref, hi_ref, cot_ref, mixer_ref, stencil_ref, out_mixer_ref, scale_ref, offset_ref,
    flag_ref, mixed_ref, proj_ref, ga_ref, gram_ref, m_ref, acc_ref,
):
    rows, channels, width = own_ref.shape
    scale = scale_ref[...]
    offset = offset_ref[...]
    mixer = mixer_ref[...]
    out_mixer = out_mixer_ref[...]

    def project(x, flag):
        standard, _ = standardized(x)
        normed = (standard * scale + offset).astype(BF16)
        p = dot(mixer, normed)
        return (p if flag is None else p * flag).astype(BF16)

    for i in range(2):
        proj_ref[i] = project(lo_ref[i], flag_ref[0])
        proj_ref[rows + 2 + i] = project(hi_ref[i], flag_ref[1])

    @pl.loop(0, rows)
    def _(r):
        proj_ref[r + 2] = project(own_ref[r], None)

    ga_ref[0] = dot(out_mixer, lo_ref[2], TN).astype(BF16)
    ga_ref[rows + 1] = dot(out_mixer, hi_ref[2], TN).astype(BF16)

    @pl.loop(0, rows)
    def _(r):
        ga_ref[r + 1] = dot(out_mixer, cot_ref[r], TN).astype(BF16)

    group = 16
    lanes = lax.broadcasted_iota(jnp.int32, (group, width), 1)

    @pl.loop(0, 3 * channels // group)
    def _(g):
        at = pl.ds(pl.multiple_of(g * group, group), group)
        weights = stencil_ref[at, :]
        w = [jnp.broadcast_to(weights[:, t : t + 1], (group, width)) for t in range(9)]
        line = [proj_ref[i, at, :].astype(F32) for i in range(2)]
        for r in range(rows + 2):
            line.append(proj_ref[r + 2, at, :].astype(F32))
            sums = [
                w[b] * line[r] + w[3 + b] * line[r + 1] + w[6 + b] * line[r + 2] for b in range(3)
            ]
            right = jnp.where(lanes == 0, 0.0, pltpu.roll(sums[0], 1, 1))
            left = jnp.where(lanes == width - 1, 0.0, pltpu.roll(sums[2], width - 1, 1))
            mixed_ref[r, at, :] = (sums[1] + right + left).astype(BF16)

    acc_ref[...] = jnp.zeros_like(acc_ref)

    @pl.loop(0, rows)
    def _(r):
        q = mixed_ref[r + 1, 0:channels, :]
        k = mixed_ref[r + 1, channels : 2 * channels, :]
        v = mixed_ref[r + 1, 2 * channels : 3 * channels, :]
        acc_ref[0] += dot(q, k, NT)
        acc_ref[1] += dot(ga_ref[r + 1], v, NT)
        acc_ref[2] += dot(cot_ref[r], v, NT)
        qf = q.astype(F32)
        kf = k.astype(F32)
        acc_ref[3, :, 0:1] += jnp.sum(qf * qf, axis=1, keepdims=True)
        acc_ref[3, :, 1:2] += jnp.sum(kf * kf, axis=1, keepdims=True)

    m_ref[...] = acc_ref[2]
    gram_ref[...] = jnp.zeros_like(gram_ref)
    heads = channels // 48
    for h in range(heads):
        a, b = 48 * h, 48 * (h + 1)
        gram_ref[a:b, 0:48] = acc_ref[0, a:b, a:b]
        gram_ref[a:b, 48:96] = acc_ref[1, a:b, a:b]
    gram_ref[0:channels, 96:98] = acc_ref[3, :, 0:2]


def backward_kernel(
    mixed_ref, proj_ref, ga_ref, gram_ref, m_ref, own_ref, cot_ref, mixer_ref, stencil_ref,
    scale_ref, sharp_ref, flag_ref, out_ref, red_ref, gg_ref, ggt_ref, at_ref, coef_ref,
    gm_ref, gp_ref, sacc_ref, extra_ref,
):
    rows, channels, width = own_ref.shape
    heads = channels // 48
    gg_ref[...] = jnp.zeros_like(gg_ref)
    ggt_ref[...] = jnp.zeros_like(ggt_ref)
    at_ref[...] = jnp.zeros_like(at_ref)
    extra_ref[...] = jnp.zeros_like(extra_ref)
    sacc_ref[...] = jnp.zeros_like(sacc_ref)
    eye = lax.broadcasted_iota(jnp.int32, (48, 48), 0) == lax.broadcasted_iota(
        jnp.int32, (48, 48), 1
    )
    lane = lax.broadcasted_iota(jnp.int32, (1, 128), 1)
    for h in range(heads):
        a, b = 48 * h, 48 * (h + 1)
        gram = gram_ref[a:b, 0:48]
        grad_att = gram_ref[a:b, 48:96]
        qsq = gram_ref[a:b, 96:97]
        ksq_col = gram_ref[a:b, 97:98]
        ksq = jnp.sum(jnp.where(eye, ksq_col, 0.0), axis=0, keepdims=True)
        lengths = jnp.sqrt(qsq + 1e-06) * jnp.sqrt(ksq + 1e-06)
        cosine = gram / lengths
        e = jnp.exp(cosine * sharp_ref[h])
        attention = e / jnp.sum(e, axis=1, keepdims=True)
        grad_scores = attention * (grad_att - jnp.sum(attention * grad_att, axis=1, keepdims=True))
        sharp_sum = jnp.sum(jnp.sum(grad_scores * cosine, axis=1, keepdims=True), axis=0, keepdims=True)
        sharp_sum = sharp_sum * flag_ref[2]
        sharp_hi = sharp_sum.astype(BF16).astype(F32)
        extra_ref[3 * channels : 3 * channels + 1, :] += jnp.where(lane == 64 + h, sharp_hi, 0.0)
        extra_ref[3 * channels : 3 * channels + 1, :] += jnp.where(
            lane == 68 + h, sharp_sum - sharp_hi, 0.0
        )
        grad_cos = grad_scores * sharp_ref[h]
        gg = grad_cos / lengths
        terms = grad_cos * cosine
        gg_ref[a:b, a:b] = gg.astype(BF16)
        ggt_ref[a:b, a:b] = gg.T.astype(BF16)
        at_ref[a:b, a:b] = attention.T.astype(BF16)
        coef_ref[a:b, 0:1] = jnp.sum(terms, axis=1, keepdims=True) / (qsq + 1e-06)
        kc = jnp.sum(terms, axis=0, keepdims=True) / (ksq + 1e-06)
        coef_ref[a:b, 1:2] = jnp.sum(jnp.where(eye, kc, 0.0), axis=1, keepdims=True)

    oma = dot(m_ref[...].astype(BF16), at_ref[...])

    qc = coef_ref[:, 0:1]
    kc = coef_ref[:, 1:2]

    def grads(r, flag):
        q = mixed_ref[r, 0:channels, :]
        k = mixed_ref[r, channels : 2 * channels, :]
        gq = dot(gg_ref[...], k) - q.astype(F32) * qc
        gk = dot(ggt_ref[...], q) - k.astype(F32) * kc
        gv = dot(at_ref[...], ga_ref[r])
        if flag is not None:
            gq, gk, gv = gq * flag, gk * flag, gv * flag
        gm_ref[r, 0:channels, :] = gq.astype(BF16)
        gm_ref[r, channels : 2 * channels, :] = gk.astype(BF16)
        gm_ref[r, 2 * channels : 3 * channels, :] = gv.astype(BF16)

    grads(0, flag_ref[0])
    grads(rows + 1, flag_ref[1])

    @pl.loop(1, rows + 1)
    def _(r):
        grads(r, None)

    group = 16
    lanes = lax.broadcasted_iota(jnp.int32, (group, width), 1)
    lane_g = lax.broadcasted_iota(jnp.int32, (group, 128), 1)

    @pl.loop(0, 3 * channels // group)
    def _(g):
        at = pl.ds(pl.multiple_of(g * group, group), group)
        weights = stencil_ref[at, :]
        w = [jnp.broadcast_to(weights[:, t : t + 1], (group, width)) for t in range(9)]
        line = [gm_ref[i, at, :].astype(F32) for i in range(2)]
        for r in range(rows):
            line.append(gm_ref[r + 2, at, :].astype(F32))
            sums = [
                w[b] * line[r + 2] + w[3 + b] * line[r + 1] + w[6 + b] * line[r] for b in range(3)
            ]
            left = jnp.where(lanes == width - 1, 0.0, pltpu.roll(sums[0], width - 1, 1))
            right = jnp.where(lanes == 0, 0.0, pltpu.roll(sums[2], 1, 1))
            gp_ref[r, at, :] = (sums[1] + right + left).astype(BF16)

    @pl.loop(0, 3 * channels // group)
    def _(g):
        at = pl.ds(pl.multiple_of(g * group, group), group)
        acc = [jnp.zeros((group, width), F32) for _ in range(9)]
        for r in range(rows):
            g_mid = gm_ref[r + 1, at, :].astype(F32)
            right, left = shifted(g_mid, lanes)
            for a in range(3):
                p = proj_ref[r + 1 + a, at, :].astype(F32)
                acc[3 * a] += p * left
                acc[3 * a + 1] += p * g_mid
                acc[3 * a + 2] += p * right
        total = jnp.zeros((group, 128), F32)
        for t in range(9):
            s = jnp.sum(acc[t], axis=1, keepdims=True)
            total = total + jnp.where(lane_g == 72 + t, s, 0.0)
        extra_ref[at, :] = total

    scale = scale_ref[...]
    mixer = mixer_ref[...]

    @pl.loop(0, rows)
    def _(r):
        standard, inverse = standardized(own_ref[r])
        gp = gp_ref[r]
        right = jnp.concatenate([standard.astype(BF16), jnp.ones((64, width), BF16)], axis=0)
        sacc_ref[...] += dot(gp, right, NT)
        scaled = dot(mixer, gp, TN) * scale
        first = jnp.mean(scaled, axis=0, keepdims=True)
        second = jnp.mean(scaled * standard, axis=0, keepdims=True)
        out_ref[r] = (
            cot_ref[r].astype(F32) + (scaled - first - standard * second) * inverse
        ).astype(BF16)

    n1 = 3 * channels
    n2 = 4 * channels
    red_ref[0:n1, :] = sacc_ref[:, 0:128].astype(BF16)
    red_ref[n1:n2, :] = oma[:, 0:128].astype(BF16)
    tail = sacc_ref[:, 128:256]
    tail_lane = lax.broadcasted_iota(jnp.int32, tail.shape, 1)
    hi = tail.astype(BF16).astype(F32)
    tail = jnp.where(tail_lane <= 64, tail, jnp.where(tail_lane == 65, tail - hi, 0.0))
    red_ref[n2 : n2 + n1, :] = (tail + extra_ref[0:n1, :]).astype(BF16)
    oma_tail = jnp.concatenate([oma[:, 128:192], jnp.zeros((channels, 64), F32)], axis=1)
    red_ref[n2 + n1 :, :] = (oma_tail + extra_ref[n1:, :]).astype(BF16)


def reduce_kernel(axes, src_ref, out_ref, recv, gath, send1, recv1, send2, recv2):
    n = src_ref.shape[0]
    me = jnp.int32(0)
    for name, size in axes:
        me = me * size + lax.axis_index(name)

    def device(p):
        ids = {}
        for name, size in reversed(axes):
            ids[name] = lax.rem(p, size)
            p = lax.div(p, size)
        return ids

    def peer(d):
        return lax.rem(me + d, n)

    barrier = pltpu.get_barrier_semaphore()

    @pl.loop(1, n)
    def _(d):
        pl.semaphore_signal(
            barrier, inc=1, device_id=device(peer(d)), device_id_type=pl.DeviceIdType.MESH
        )

    pl.semaphore_wait(barrier, n - 1)

    @pl.loop(1, n)
    def _(d):
        p = peer(d)
        pltpu.make_async_remote_copy(
            src_ref=src_ref.at[p], dst_ref=recv.at[me], send_sem=send1, recv_sem=recv1,
            device_id=device(p), device_id_type=pl.DeviceIdType.MESH,
        ).start()

    recv[me] = src_ref[me]
    all_but_one = pl.ds(0, n - 1)
    pltpu.make_async_copy(recv.at[all_but_one], recv.at[all_but_one], recv1).wait()

    def add(i, acc):
        return acc + recv[i].astype(F32)

    total = lax.fori_loop(0, n, add, jnp.zeros(src_ref.shape[1:], F32))
    gath[me] = total.astype(gath.dtype)

    @pl.loop(1, n)
    def _(d):
        p = peer(d)
        pltpu.make_async_remote_copy(
            src_ref=gath.at[me], dst_ref=gath.at[me], send_sem=send2, recv_sem=recv2,
            device_id=device(p), device_id_type=pl.DeviceIdType.MESH,
        ).start()

    pltpu.make_async_copy(gath.at[all_but_one], gath.at[all_but_one], recv2).wait()
    out_ref[...] = gath[...]
    pltpu.make_async_copy(gath.at[all_but_one], gath.at[all_but_one], send2).wait()
    pltpu.make_async_copy(recv.at[all_but_one], recv.at[all_but_one], send1).wait()


def all_reduce(x, axes, tile_rows, collective_id):
    axes = tuple((name, lax.axis_size(name)) for name in axes)
    n = 1
    for _, size in axes:
        n *= size
    rows = x.shape[0]
    each = -(-rows // (n * tile_rows)) * tile_rows
    if each * n != rows:
        x = jnp.pad(x, ((0, each * n - rows), (0, 0)))
    x = x.reshape(n, each, 128)
    slots = pltpu.VMEM((n, each, 128), x.dtype)
    sem = pltpu.SemaphoreType.DMA
    out = pl.pallas_call(
        functools.partial(reduce_kernel, axes),
        out_shape=jax.ShapeDtypeStruct(x.shape, x.dtype),
        in_specs=[VMEM],
        out_specs=VMEM,
        scratch_shapes=[slots, slots, sem, sem, sem, sem],
        compiler_params=pltpu.CompilerParams(
            collective_id=collective_id, has_side_effects=True, vmem_limit_bytes=LIMIT
        ),
        name=f"all_reduce_{collective_id}",
    )(x)
    return out.reshape(n * each, 128)[:rows]


def local(
    block_feature_map, upstream_sensitivity, triple_mixer, spatial_stencil, outgoing_mixer,
    sharpness_factor, standardize_scaling, standardize_offset,
):
    _, channels, rows, width = block_feature_map.shape
    heads = sharpness_factor.shape[0]
    n = lax.axis_size("tile")
    me = lax.axis_index("tile")
    own = jnp.transpose(block_feature_map[0], (1, 0, 2))
    cot = jnp.transpose(upstream_sensitivity[0], (1, 0, 2))
    up = [(i, i + 1) for i in range(n - 1)]
    down = [(j, i) for i, j in up]
    last = jnp.concatenate([own[rows - 2 :], cot[rows - 1 :]], axis=0)
    first = jnp.concatenate([own[:2], cot[:1]], axis=0)
    lo = lax.ppermute(last, "tile", up)
    hi = lax.ppermute(first, "tile", down)
    flags = jnp.stack([me > 0, me < n - 1, me == 0]).astype(F32)
    stencil = spatial_stencil.reshape(3 * channels, 9)
    scale = standardize_scaling.reshape(channels, 1)
    offset = standardize_offset.reshape(channels, 1)

    params = pltpu.CompilerParams(vmem_limit_bytes=LIMIT)
    shape = jax.ShapeDtypeStruct
    mixed, proj, ga, gram, m = pl.pallas_call(
        forward_kernel,
        out_shape=(
            shape((rows + 2, 3 * channels, width), BF16),
            shape((rows + 4, 3 * channels, width), BF16),
            shape((rows + 2, channels, width), BF16),
            shape((channels, 128), F32),
            shape((channels, channels), F32),
        ),
        in_specs=[VMEM] * 9 + [SMEM],
        out_specs=[VMEM] * 5,
        scratch_shapes=[pltpu.VMEM((4, channels, channels), F32)],
        compiler_params=params,
        name="forward",
    )(lo, own, hi, cot, triple_mixer, stencil, outgoing_mixer, scale, offset, flags)

    gram = all_reduce(gram, ("tile",), 8, 1)

    out, red = pl.pallas_call(
        backward_kernel,
        out_shape=(
            shape((rows, channels, width), BF16),
            shape((8 * channels, 128), BF16),
        ),
        in_specs=[VMEM] * 10 + [SMEM] * 2,
        out_specs=[VMEM] * 2,
        scratch_shapes=[
            pltpu.VMEM((channels, channels), BF16),
            pltpu.VMEM((channels, channels), BF16),
            pltpu.VMEM((channels, channels), BF16),
            pltpu.VMEM((channels, 128), F32),
            pltpu.VMEM((rows + 2, 3 * channels, width), BF16),
            pltpu.VMEM((rows, 3 * channels, width), BF16),
            pltpu.VMEM((3 * channels, 256), F32),
            pltpu.VMEM((4 * channels, 128), F32),
        ],
        compiler_params=params,
        name="backward",
    )(mixed, proj, ga, gram, m, own, cot, triple_mixer, stencil, scale, sharpness_factor, flags)

    red = all_reduce(red, ("img", "tile"), 16, 2).astype(F32)
    n1 = 3 * channels
    left, right = red[: 4 * channels], red[4 * channels :]
    s = jnp.concatenate([left[:n1], right[:n1, :64]], axis=1)
    gsum = right[:n1, 64:65] + right[:n1, 65:66]
    triple_adjoint = s * standardize_scaling[None, :] + gsum * standardize_offset[None, :]
    mixer = triple_mixer.astype(F32)
    return (
        jnp.transpose(out, (1, 0, 2))[None],
        triple_adjoint,
        right[:n1, 72:81].reshape(n1, 3, 3),
        jnp.concatenate([left[n1:], right[n1:, :64]], axis=1),
        right[n1, 64 : 64 + heads] + right[n1, 68 : 68 + heads],
        jnp.sum(mixer * s, axis=0),
        jnp.sum(mixer * gsum, axis=0),
    )


def solution(mesh):
    rows = P("img", None, "tile", None)
    return jax.shard_map(
        local,
        mesh=mesh,
        in_specs=(rows, rows, P(), P(), P(), P(), P(), P()),
        out_specs=(rows, P(), P(), P(), P(), P(), P()),
        check_vma=False,
    )
```

time: 357 us -> 117 us (0.33)
  waiting for transfers between devices: 183 us -> 0.34 us
  Pallas kernels: 0 us -> 93.6 us
  other arithmetic: 55.6 us -> 4.8 us
  blocking collectives: 48.1 us -> 0 us
  matrix products: 22 us -> 0 us
  between operations: 14.6 us -> 0.84 us
  local copies, waits for them, and re-layouts: 24.2 us -> 13.7 us
  starting transfers between devices: 8.13 us -> 3.67 us
    psum x2 -> x0, waiting for transfers between devices: 179 us -> none  [the longest x1 93.8 us: local(): gram_raw, query_sq, key_sq = lax.psum((gram_raw, query_sq, key_sq), 'tile')]
    pallas_call x0 -> x4, Pallas kernels: none -> 93.6 us  [the longest x2 44.9 us: all_reduce(): pl.pallas_call(functools.partial(reduce_kernel, axes), out_shape=jax.Shap...]
    psum x1 -> x0, blocking collectives: 48.1 us -> none  [local(): lax.psum((triple_mixer_adjoint, spatial_stencil_adjoint, outgoing_mixer_a...]
    dot_general x11 -> x0, matrix products: 22 us -> none  [the longest x1 9.72 us: local(): jnp.einsum('bop,bcp->oc', flat_gproj, normed.reshape(images, channels, pi...]
    reduce_sum x9 -> x1, other arithmetic: 20.5 us -> 1.49 us  [local(): jnp.sum(mixer * gsum, axis=0)]
    unnamed x2 -> x0, other arithmetic: 18.9 us -> none
    convert_element_type x5 -> x2, other arithmetic: 12.4 us -> 1.64 us  [the longest x1 1.05 us: local(): red = all_reduce(red, ('img', 'tile'), 16, 2).astype(F32)]
    unnamed x36 -> x20, local copies, waits for them, and re-layouts: 12 us -> 3.36 us
  transfers between devices with their start and end apart: 6 -> 2, of which waited for: 3 -> 1; matrix products, arithmetic and copies ran while one was open for 1% -> 3% of each run, Pallas kernels for 0% -> 0%
where the time goes in v1:
time: 117 us
  Pallas kernels  93.6 us (80%)
  local copies, waits for them, and re-layouts  13.7 us (12%)
  other arithmetic  4.8 us (4%)
  starting transfers between devices  3.67 us (3%)
    pallas_call x2, Pallas kernels, all_reduce(): pl.pallas_call(functools.partial(reduce_kernel, axes), out_shape=jax.Shap...  44.9 us
    pallas_call x1, Pallas kernels, local(): pl.pallas_call(backward_kernel, out_shape=(shape((rows, channels, width),...  28.3 us
    pallas_call x1, Pallas kernels, local(): pl.pallas_call(forward_kernel, out_shape=(shape((rows + 2, 3 * channels,...  20.4 us
    unnamed x20, local copies, waits for them, and re-layouts  3.36 us
    ppermute x1, starting transfers between devices, local(): lo = lax.ppermute(last, 'tile', up)  2.37 us
  transfers between devices with their start and end apart: 2, of which 1 were waited for; matrix products, arithmetic and copies ran while one was open for 3% of the time, Pallas kernels for 0%

profile of v1, /device:TPU:0, one launch (start us, length us, event | category | flops | bytes accessed | tf_op | source)
XLA Modules:
  0.0 116.9 jit_solution(16869681549637083743)
XLA Ops:
  0.7 1.8 %copy_bitcast_fusion = (bf16[8,192,256]{2,1,0:T(8,128)(2,1)S(1)}, bf16[8,192,256]{2,1,0:T(8,128)(2,1)S(1)}) fusion(bf16[1,192,8,256]{3,2,1,0:T(8,128)(2,1)} %param.9, bf16[1,192,8,256]{3,2,1,0:T(8,128)(2,1)} %param.8), kind=kLoop, calls=%fused_computation | loop fusion | bytes 3145728 | tf_op jit(solution)/shard_map/transpose | solution.py:339
  2.4 0.0 copy-start
  2.6 2.4 %collective-permute-start = (bf16[3,192,256]{2,1,0:T(8,128)(2,1)S(1)}, bf16[3,192,256]{2,1,0:T(8,128)(2,1)S(1)}, u32[]{:S(2)}, u32[]{:S(2)}) collective-permute-start(bf16[3,192,256]{2,1,0:T(8,128)(2,1)S(1)} %pad_maximum_fusion.1), channel_id=1, source_target_pairs={{0,1},{1,2},{2,3},{3,4},{4,5},{5,6},{6,7},{7,8},{8,9},{9,10},{10,1... | collective-permute-start | bytes 884744 | tf_op jit(solution)/shard_map/ppermute | solution.py:344
  5.0 1.3 %collective-permute-start.1 = (bf16[3,192,256]{2,1,0:T(8,128)(2,1)S(1)}, bf16[3,192,256]{2,1,0:T(8,128)(2,1)S(1)}, u32[]{:S(2)}, u32[]{:S(2)}) collective-permute-start(bf16[3,192,256]{2,1,0:T(8,128)(2,1)S(1)} %pad_maximum_fusion.2), channel_id=1, source_target_pairs={{1,0},{2,1},{3,2},{4,3},{5,4},{6,5},{7,6},{8,7},{9,8},{10,9},{11,1... | collective-permute-start | bytes 884744 | tf_op jit(solution)/shard_map/ppermute | solution.py:345
  6.3 0.8 copy.27.scale_ref
  7.1 0.8 copy.28.offset_ref
  7.9 0.9 copy.26.stencil_ref
  8.7 0.9 copy.25.mixer_ref
  9.6 0.6 add_convert_fusion.flag_ref
  10.2 0.0 collective-permute-done.lo_ref
  10.2 0.3 collective-permute-done.1.hi_ref
  10.6 0.4 copy-done.4
  10.9 0.7 copy-done.5
  11.7 20.4 %forward.1 = (bf16[10,576,256]{2,1,0:T(8,128)(2,1)}, bf16[12,576,256]{2,1,0:T(8,128)(2,1)}, bf16[10,192,256]{2,1,0:T(8,128)(2,1)}, f32[192,128]{1,0:T(8,128)}, f32[192,192]{1,0:T(8,128)}) custom-call(bf16[3,192,256]{2,1,0:T(8,128)(2,1)} %copy-done.4, bf16[8,192,256]{2,1,0:T(8,128)(2,1)} %copy-done, bf16[3,192,256]{2,1,0:T(8,128)(2,1)} %copy-done.5, ...), custom_call_target="tpu_custom_call" | custom-call | tf_op jit(solution)/shard_map/forward/pallas_call | solution.py:353
  32.1 1.6 %pad.4 = f32[256,128]{1,0:T(8,128)} pad(f32[192,128]{1,0:T(8,128)} %get-tuple-element.17, f32[]{:T(128)} %constant.10.clone.1), padding=0_64x0_0 | pad | bytes 229380 | tf_op jit(solution)/shard_map/jit(_pad)/pad | solution.py:312
  33.7 19.9 %all_reduce_1.1 = f32[16,16,128]{2,1,0:T(8,128)} custom-call(f32[16,16,128]{2,1,0:T(8,128)} %bitcast.35), custom_call_target="tpu_custom_call" | custom-call | tf_op jit(solution)/shard_map/all_reduce_1/pallas_call | solution.py:316
  53.6 1.5 %slice.66 = f32[12,16,128]{2,1,0:T(8,128)} slice(f32[16,16,128]{2,1,0:T(8,128)} %all_reduce_1.1), slice={[0:12], [0:16], [0:128]} | slice | bytes 196608 | tf_op jit(solution)/shard_map/slice | solution.py:327
  55.2 28.3 %backward.1 = (bf16[8,192,256]{2,1,0:T(8,128)(2,1)}, bf16[1536,128]{1,0:T(8,128)(2,1)}) custom-call(bf16[10,576,256]{2,1,0:T(8,128)(2,1)} %get-tuple-element.14.mixed_ref, bf16[12,576,256]{2,1,0:T(8,128)(2,1)} %get-tuple-element.15.proj_ref, bf16[10,192,256]{2,1,0:T(8,128)(2,1)} %get-tuple-element.16.ga_ref, f32[192,128]{1,0:T(8,128)} %bitcast.38, ...), custom_call_target="tpu_custom_call" | custom-call | tf_op jit(solution)/shard_map/backward/pallas_call | solution.py:371
  83.5 25.0 %all_reduce_2.1 = bf16[32,48,128]{2,1,0:T(8,128)(2,1)} custom-call(bf16[32,48,128]{2,1,0:T(8,128)(2,1)} %bitcast.36), custom_call_target="tpu_custom_call" | custom-call | tf_op jit(solution)/shard_map/all_reduce_2/pallas_call | solution.py:316
  108.4 0.8 slice.88
  109.2 0.9 slice.83
  110.2 1.0 convert_element_type.15
  111.2 0.6 fusion.3
  111.8 0.3 fusion.2
  112.2 0.1 slice.87
  112.3 1.3 %copy.35 = bf16[1,192,8,256]{3,2,1,0:T(8,128)(2,1)} copy(bf16[1,192,8,256]{3,1,2,0:T(8,128)(2,1)S(1)} %bitcast.34) | data formatting | bytes 1572864
  113.6 0.2 copy.32
  113.8 0.1 copy.34
  113.9 0.2 copy.33
  114.1 0.6 reshape.46
  114.7 0.7 pad_maximum_fusion.3
  115.4 1.5 %fusion.1 = (f32[192]{0:T(256)}, f32[192]{0:T(256)}, f32[576,192]{0,1:T(8,128)}) fusion(bf16[576,192]{0,1:T(8,128)(2,1)S(1)} %copy-done.2, f32[576]{0:T(1024)S(1)} %fusion.2, f32[576,64]{0,1:T(8,128)S(1)} %copy.33, f32[576,128]{0,1:T(8,128)S(1)} %copy.32, f32[192]{0:T(256)S(1)} %copy-done.8, f32[192]{0:T(256)S(1)} %copy-done.7), kind=kLoop, calls=%fused_computation.5 | loop fusion | flops 994944 | bytes 1111296 | tf_op jit(solution)/shard_map/reduce_sum | solution.py:407
  (22 shorter events, 0.2 us)
Async XLA Ops:
  0.6 5.7 %copy-start.6 = (f32[576,3,3]{0,2,1:T(4,128)S(1)}, f32[576,3,3]{0,2,1:T(4,128)}, u32[]{:S(2)}) copy-start(f32[576,3,3]{0,2,1:T(4,128)} %param.11) | copy-start | bytes 62212
  0.6 5.7 %copy-start.7 = (f32[192]{0:T(256)S(1)}, f32[192]{0:T(256)}, u32[]{:S(2)}) copy-start(f32[192]{0:T(256)} %param.14) | copy-start | bytes 2308
  0.7 6.4 %copy-start.8 = (f32[192]{0:T(256)S(1)}, f32[192]{0:T(256)}, u32[]{:S(2)}) copy-start(f32[192]{0:T(256)} %param.15) | copy-start | bytes 2308
  0.7 8.1 %copy-start.2 = (bf16[576,192]{0,1:T(8,128)(2,1)S(1)}, bf16[576,192]{0,1:T(8,128)(2,1)}, u32[]{:S(2)}) copy-start(bf16[576,192]{0,1:T(8,128)(2,1)} %param.10) | copy-start | bytes 663556
  2.4 8.1 %copy-start = (bf16[8,192,256]{2,1,0:T(8,128)(2,1)}, bf16[8,192,256]{2,1,0:T(8,128)(2,1)S(1)}, u32[]{:S(2)}) copy-start(bf16[8,192,256]{2,1,0:T(8,128)(2,1)S(1)} %get-tuple-element.43.own_ref) | copy-start | bytes 2359300
  2.5 8.1 %copy-start.1 = (bf16[8,192,256]{2,1,0:T(8,128)(2,1)}, bf16[8,192,256]{2,1,0:T(8,128)(2,1)S(1)}, u32[]{:S(2)}) copy-start(bf16[8,192,256]{2,1,0:T(8,128)(2,1)S(1)} %get-tuple-element.42.cot_ref) | copy-start | bytes 2359300
  2.6 7.7 %collective-permute-start = (bf16[3,192,256]{2,1,0:T(8,128)(2,1)S(1)}, bf16[3,192,256]{2,1,0:T(8,128)(2,1)S(1)}, u32[]{:S(2)}, u32[]{:S(2)}) collective-permute-start(bf16[3,192,256]{2,1,0:T(8,128)(2,1)S(1)} %pad_maximum_fusion.1), channel_id=1, source_target_pairs={{0,1},{1,2},{2,3},{3,4},{4,5},{5,6},{6,7},{7,8},{8,9},{9,10},{10,1... | collective-permute-start | bytes 884744 | tf_op jit(solution)/shard_map/ppermute | solution.py:344
  5.0 5.6 %collective-permute-start.1 = (bf16[3,192,256]{2,1,0:T(8,128)(2,1)S(1)}, bf16[3,192,256]{2,1,0:T(8,128)(2,1)S(1)}, u32[]{:S(2)}, u32[]{:S(2)}) collective-permute-start(bf16[3,192,256]{2,1,0:T(8,128)(2,1)S(1)} %pad_maximum_fusion.2), channel_id=1, source_target_pairs={{1,0},{2,1},{3,2},{4,3},{5,4},{6,5},{7,6},{8,7},{9,8},{10,9},{11,1... | collective-permute-start | bytes 884744 | tf_op jit(solution)/shard_map/ppermute | solution.py:345
  10.2 0.7 copy-start.4
  10.9 0.7 copy-start.5
  83.5 28.9 %copy-start.3 = (bf16[8,192,256]{2,1,0:T(8,128)(2,1)S(1)}, bf16[8,192,256]{2,1,0:T(8,128)(2,1)}, u32[]{:S(2)}) copy-start(bf16[8,192,256]{2,1,0:T(8,128)(2,1)} %get-tuple-element.19) | copy-start | bytes 2359300

commit v2 on v1

v2 whole, which is shorter than its diff:
```python
import functools
import jax
import jax.numpy as jnp
from jax import lax
from jax.experimental import pallas as pl
from jax.experimental.pallas import tpu as pltpu
from jax.sharding import PartitionSpec as P

F32 = jnp.float32
BF16 = jnp.bfloat16
NT = (((1,), (1,)), ((), ()))
NN = (((1,), (0,)), ((), ()))
TN = (((0,), (0,)), ((), ()))
VMEM = pl.BlockSpec(memory_space=pltpu.VMEM)
SMEM = pl.BlockSpec(memory_space=pltpu.SMEM)
LIMIT = 56 * 1024 * 1024


def dot(a, b, dims=NN):
    return lax.dot_general(a, b, dims, preferred_element_type=F32)


def standardized(x):
    xf = x.astype(F32)
    centered = xf - jnp.mean(xf, axis=0, keepdims=True)
    inverse = lax.rsqrt(jnp.mean(centered * centered, axis=0, keepdims=True) + 1e-05)
    return centered * inverse, inverse


def shifted(v, lanes):
    width = v.shape[-1]
    right = jnp.where(lanes == 0, 0.0, pltpu.roll(v, 1, 1))
    left = jnp.where(lanes == width - 1, 0.0, pltpu.roll(v, width - 1, 1))
    return right, left


def column(row):
    n = row.shape[1]
    eye = lax.broadcasted_iota(jnp.int32, (n, n), 0) == lax.broadcasted_iota(jnp.int32, (n, n), 1)
    return jnp.sum(jnp.where(eye, row, 0.0), axis=1, keepdims=True)


def remote(src, dst, sems, ids):
    return pltpu.make_async_remote_copy(
        src_ref=src, dst_ref=dst, send_sem=sems.at[0], recv_sem=sems.at[1], device_id=ids,
        device_id_type=pl.DeviceIdType.MESH,
    )


def wait_bytes(ref, sem):
    pltpu.make_async_copy(ref, ref, sem).wait()


def kernel(
    n_img, n_tile,
    own_ref, cot_ref, mixer_ref, stencil_ref, out_mixer_ref, scale_ref, offset_ref, sharp_ref,
    out_ref, triple_ref, stencil_out_ref, outgoing_ref, sharp_out_ref, scaling_ref, offset_out_ref,
    lo, hi, proj, mixed, ga, gm, gp, acc, gram, gram_recv, gram_all, gg_ref, ggt_ref, at_ref, coef,
    sacc, extra, red, pair, half, recv, gath,
    lo_x, lo_c, hi_x, hi_c, gram_rs, gram_ag, pair_rs, main_rs, main_ag, pair_ag,
):
    rows, channels, width = own_ref.shape
    heads = channels // 48
    img = lax.axis_index("img")
    tile = lax.axis_index("tile")
    n = n_img * n_tile
    me = img * n_tile + tile

    def device(p):
        return {"img": lax.div(p, n_tile), "tile": lax.rem(p, n_tile)}

    barrier = pltpu.get_barrier_semaphore()

    @pl.loop(1, n)
    def _(d):
        pl.semaphore_signal(
            barrier, inc=1, device_id=device(lax.rem(me + d, n)),
            device_id_type=pl.DeviceIdType.MESH,
        )

    pl.semaphore_wait(barrier, n - 1)

    def to_next():
        ids = {"img": img, "tile": tile + 1}
        return (
            remote(own_ref.at[pl.ds(rows - 2, 2)], lo.at[pl.ds(0, 2)], lo_x, ids),
            remote(cot_ref.at[pl.ds(rows - 1, 1)], lo.at[pl.ds(2, 1)], lo_c, ids),
        )

    def to_previous():
        ids = {"img": img, "tile": tile - 1}
        return (
            remote(own_ref.at[pl.ds(0, 2)], hi.at[pl.ds(0, 2)], hi_x, ids),
            remote(cot_ref.at[pl.ds(0, 1)], hi.at[pl.ds(2, 1)], hi_c, ids),
        )

    has_lo = tile > 0
    has_hi = tile < n_tile - 1

    @pl.when(has_hi)
    def _():
        for copy in to_next():
            copy.start()

    @pl.when(has_lo)
    def _():
        for copy in to_previous():
            copy.start()

    scale = column(scale_ref[...])
    offset = column(offset_ref[...])
    mixer = mixer_ref[...]
    out_mixer = out_mixer_ref[...]

    def project(x):
        standard, _ = standardized(x)
        normed = (standard * scale + offset).astype(BF16)
        return dot(mixer, normed).astype(BF16)

    @pl.loop(0, rows, unroll=2)
    def _(r):
        proj[r + 2] = project(own_ref[r])
        ga[r + 1] = dot(out_mixer, cot_ref[r], TN).astype(BF16)

    @pl.when(has_lo)
    def _():
        for copy in to_next():
            copy.wait_recv()
        for i in range(2):
            proj[i] = project(lo[i])
        ga[0] = dot(out_mixer, lo[2], TN).astype(BF16)

    @pl.when(jnp.logical_not(has_lo))
    def _():
        proj[0:2] = jnp.zeros((2,) + proj.shape[1:], BF16)
        ga[0] = jnp.zeros(ga.shape[1:], BF16)

    @pl.when(has_hi)
    def _():
        for copy in to_previous():
            copy.wait_recv()
        for i in range(2):
            proj[rows + 2 + i] = project(hi[i])
        ga[rows + 1] = dot(out_mixer, hi[2], TN).astype(BF16)

    @pl.when(jnp.logical_not(has_hi))
    def _():
        proj[rows + 2 : rows + 4] = jnp.zeros((2,) + proj.shape[1:], BF16)
        ga[rows + 1] = jnp.zeros(ga.shape[1:], BF16)

    group = 16
    lanes = lax.broadcasted_iota(jnp.int32, (group, width), 1)

    @pl.loop(0, 3 * channels // group)
    def _(g):
        at = pl.ds(pl.multiple_of(g * group, group), group)
        weights = stencil_ref[at, :]
        w = [jnp.broadcast_to(weights[:, t : t + 1], (group, width)) for t in range(9)]
        line = [proj[i, at, :].astype(F32) for i in range(2)]
        for r in range(rows + 2):
            line.append(proj[r + 2, at, :].astype(F32))
            sums = [
                w[b] * line[r] + w[3 + b] * line[r + 1] + w[6 + b] * line[r + 2] for b in range(3)
            ]
            right = jnp.where(lanes == 0, 0.0, pltpu.roll(sums[0], 1, 1))
            left = jnp.where(lanes == width - 1, 0.0, pltpu.roll(sums[2], width - 1, 1))
            mixed[r, at, :] = (sums[1] + right + left).astype(BF16)

    acc[...] = jnp.zeros_like(acc)

    @pl.loop(0, rows, unroll=2)
    def _(r):
        q = mixed[r + 1, 0:channels, :]
        k = mixed[r + 1, channels : 2 * channels, :]
        v = mixed[r + 1, 2 * channels : 3 * channels, :]
        acc[0, :, 0:channels] += dot(q, k, NT)
        acc[1, :, 0:channels] += dot(ga[r + 1], v, NT)
        acc[2, :, 0:channels] += dot(cot_ref[r], v, NT)
        qf = q.astype(F32)
        kf = k.astype(F32)
        acc[3] += qf * qf
        acc[4] += kf * kf

    each = gram.shape[1]
    owners = gram.shape[0]
    gram_rows = owners * each
    pieces = []
    for h in range(heads):
        a, b = 48 * h, 48 * (h + 1)
        qsq = jnp.sum(acc[3, a:b, :], axis=1, keepdims=True)
        ksq = jnp.sum(acc[4, a:b, :], axis=1, keepdims=True)
        pieces.append(
            jnp.concatenate(
                [acc[0, a:b, a:b], acc[1, a:b, a:b], qsq, ksq, jnp.zeros((48, 30), F32)], axis=1,
            )
        )
    if gram_rows > channels:
        pieces.append(jnp.zeros((gram_rows - channels, 128), F32))
    packed = jnp.concatenate(pieces, axis=0)
    for i in range(owners):
        gram[i] = packed[i * each : (i + 1) * each]

    owner = tile < owners
    rest = pl.ds(0, n_tile - 1)

    @pl.loop(1, n_tile)
    def _(d):
        p = lax.rem(tile + d, n_tile)

        @pl.when(p < owners)
        def _():
            remote(gram.at[p], gram_recv.at[tile], gram_rs, {"img": img, "tile": p}).start()

    @pl.when(owner)
    def _():
        gram_recv[tile] = gram[tile]
        wait_bytes(gram_recv.at[rest], gram_rs.at[1])

        def add_gram(i, total):
            return total + gram_recv[i]

        gram_all[tile] = lax.fori_loop(0, n_tile, add_gram, jnp.zeros(gram.shape[1:], F32))

        @pl.loop(1, n_tile)
        def _(d):
            p = lax.rem(tile + d, n_tile)
            remote(gram_all.at[tile], gram_all.at[tile], gram_ag, {"img": img, "tile": p}).start()

    gg_ref[...] = jnp.zeros_like(gg_ref)
    ggt_ref[...] = jnp.zeros_like(ggt_ref)
    at_ref[...] = jnp.zeros_like(at_ref)
    extra[...] = jnp.zeros_like(extra)
    sacc[...] = jnp.zeros_like(sacc)

    @pl.when(owner)
    def _():
        wait_bytes(gram_all.at[pl.ds(0, owners - 1)], gram_ag.at[1])

    @pl.when(jnp.logical_not(owner))
    def _():
        wait_bytes(gram_all, gram_ag.at[1])

    whole = jnp.concatenate([gram_all[i] for i in range(owners)], axis=0)

    eye = lax.broadcasted_iota(jnp.int32, (48, 48), 0) == lax.broadcasted_iota(
        jnp.int32, (48, 48), 1
    )
    lane = lax.broadcasted_iota(jnp.int32, (1, 128), 1)
    leading = (tile == 0).astype(F32)
    for h in range(heads):
        a, b = 48 * h, 48 * (h + 1)
        gram_raw = whole[a:b, 0:48]
        grad_att = whole[a:b, 48:96]
        qsq = whole[a:b, 96:97]
        ksq_col = whole[a:b, 97:98]
        ksq = jnp.sum(jnp.where(eye, ksq_col, 0.0), axis=0, keepdims=True)
        lengths = jnp.sqrt(qsq + 1e-06) * jnp.sqrt(ksq + 1e-06)
        cosine = gram_raw / lengths
        e = jnp.exp(cosine * sharp_ref[h])
        attention = e / jnp.sum(e, axis=1, keepdims=True)
        grad_scores = attention * (grad_att - jnp.sum(attention * grad_att, axis=1, keepdims=True))
        sharp_sum = leading * jnp.sum(
            jnp.sum(grad_scores * cosine, axis=1, keepdims=True), axis=0, keepdims=True
        )
        extra[3 * channels : 3 * channels + 1, :] += jnp.where(lane == 64 + h, sharp_sum, 0.0)
        grad_cos = grad_scores * sharp_ref[h]
        gg = grad_cos / lengths
        terms = grad_cos * cosine
        gg_ref[a:b, a:b] = gg.astype(BF16)
        ggt_ref[a:b, a:b] = gg.T.astype(BF16)
        at_ref[a:b, a:b] = attention.T.astype(BF16)
        coef[a:b, 0:1] = jnp.sum(terms, axis=1, keepdims=True) / (qsq + 1e-06)
        kc = jnp.sum(terms, axis=0, keepdims=True) / (ksq + 1e-06)
        coef[a:b, 1:2] = jnp.sum(jnp.where(eye, kc, 0.0), axis=1, keepdims=True)

    oma = dot(acc[2, :, 0:channels].astype(BF16), at_ref[...])

    qc = coef[:, 0:1]
    kc = coef[:, 1:2]

    @pl.loop(0, rows + 2, unroll=2)
    def _(r):
        inside = jnp.logical_and(
            jnp.logical_or(r > 0, has_lo), jnp.logical_or(r < rows + 1, has_hi)
        ).astype(F32)
        q = mixed[r, 0:channels, :]
        k = mixed[r, channels : 2 * channels, :]
        gq = dot(gg_ref[...], k) - q.astype(F32) * qc
        gk = dot(ggt_ref[...], q) - k.astype(F32) * kc
        gv = dot(at_ref[...], ga[r])
        gm[r, 0:channels, :] = (gq * inside).astype(BF16)
        gm[r, channels : 2 * channels, :] = (gk * inside).astype(BF16)
        gm[r, 2 * channels : 3 * channels, :] = (gv * inside).astype(BF16)

    lane_g = lax.broadcasted_iota(jnp.int32, (group, 128), 1)

    @pl.loop(0, 3 * channels // group)
    def _(g):
        at = pl.ds(pl.multiple_of(g * group, group), group)
        weights = stencil_ref[at, :]
        w = [jnp.broadcast_to(weights[:, t : t + 1], (group, width)) for t in range(9)]
        line = [gm[i, at, :].astype(F32) for i in range(2)]
        for r in range(rows):
            line.append(gm[r + 2, at, :].astype(F32))
            sums = [
                w[b] * line[r + 2] + w[3 + b] * line[r + 1] + w[6 + b] * line[r] for b in range(3)
            ]
            left = jnp.where(lanes == width - 1, 0.0, pltpu.roll(sums[0], width - 1, 1))
            right = jnp.where(lanes == 0, 0.0, pltpu.roll(sums[2], 1, 1))
            gp[r, at, :] = (sums[1] + right + left).astype(BF16)

    @pl.loop(0, 3 * channels // group)
    def _(g):
        at = pl.ds(pl.multiple_of(g * group, group), group)
        tap = [jnp.zeros((group, width), F32) for _ in range(9)]
        line = [proj[1 + i, at, :].astype(F32) for i in range(2)]
        for r in range(rows):
            line.append(proj[r + 3, at, :].astype(F32))
            g_mid = gm[r + 1, at, :].astype(F32)
            right, left = shifted(g_mid, lanes)
            for a in range(3):
                tap[3 * a] += line[r + a] * left
                tap[3 * a + 1] += line[r + a] * g_mid
                tap[3 * a + 2] += line[r + a] * right
        total = jnp.zeros((group, 128), F32)
        for t in range(9):
            s = jnp.sum(tap[t], axis=1, keepdims=True)
            total = total + jnp.where(lane_g == 72 + t, s, 0.0)
        extra[at, :] = total

    @pl.loop(0, rows, unroll=2)
    def _(r):
        standard, _ = standardized(own_ref[r])
        ext = jnp.concatenate([standard.astype(BF16), jnp.ones((64, width), BF16)], axis=0)
        sacc[...] += dot(gp[r], ext, NT)

    n1 = 3 * channels
    n2 = 4 * channels
    groups, piece = half.shape[:2]
    tail = sacc[:, 128:256]
    tail_lane = lax.broadcasted_iota(jnp.int32, tail.shape, 1)
    tail = jnp.where(tail_lane <= 64, tail, 0.0)
    mixer_f = mixer_ref[...].astype(F32)
    scaling_part = jnp.sum(mixer_f * sacc[:, 0:channels], axis=0, keepdims=True)
    oma_lane = lax.broadcasted_iota(jnp.int32, (channels, 128), 1)
    oma_tail = jnp.concatenate([oma[:, 128:192], jnp.zeros((channels, 64), F32)], axis=1)
    oma_tail = oma_tail + jnp.where(oma_lane == 72, column(scaling_part), 0.0)

    def split_again(x):
        at = lax.broadcasted_iota(jnp.int32, x.shape, x.ndim - 1)
        both = x + pltpu.roll(x, 96, x.ndim - 1)
        high = both.astype(BF16).astype(F32)
        low = pltpu.roll(both - high, 32, x.ndim - 1)
        return jnp.where(at < 64, x, jnp.where(at < 96, high, low))

    spare = groups * piece - n2
    filler = [jnp.zeros((spare, 128), BF16)] if spare else []
    head_part = [sacc[:, 0:128].astype(BF16), oma[:, 0:128].astype(BF16)] + filler
    tail_part = [
        split_again(tail + extra[0:n1, :]).astype(BF16),
        split_again(oma_tail + extra[n1:, :]).astype(BF16),
    ] + filler
    red[0] = jnp.concatenate(head_part, axis=0).reshape(half.shape)
    red[1] = jnp.concatenate(tail_part, axis=0).reshape(half.shape)

    core = lax.rem(tile, 2)
    place = lax.div(me, 2)
    partner = {"img": img, "tile": tile + 1 - 2 * core}
    others = pl.ds(0, groups - 1)

    swap = remote(red.at[1 - core], pair, pair_rs, partner)
    swap.start()
    swap.wait_recv()

    def rounded(x):
        return jnp.where(core == 1, split_again(x), x).astype(BF16)

    def add_pair(i, _):
        half[i] = rounded(red[core, i].astype(F32) + pair[i].astype(F32))
        return 0

    lax.fori_loop(0, groups, add_pair, 0)

    @pl.loop(1, groups)
    def _(d):
        p = lax.rem(place + d, groups)
        remote(half.at[p], recv.at[place], main_rs, device(2 * p + core)).start()

    recv[place] = half[place]

    @pl.loop(0, rows, unroll=2)
    def _(r):
        standard, inverse = standardized(own_ref[r])
        scaled = dot(mixer, gp[r], TN) * scale
        first = jnp.mean(scaled, axis=0, keepdims=True)
        second = jnp.mean(scaled * standard, axis=0, keepdims=True)
        out_ref[r] = (
            cot_ref[r].astype(F32) + (scaled - first - standard * second) * inverse
        ).astype(BF16)

    wait_bytes(recv.at[others], main_rs.at[1])

    def add(i, total):
        return total + recv[i].astype(F32)

    total = lax.fori_loop(0, groups, add, jnp.zeros(recv.shape[1:], F32))
    gath[core, place] = rounded(total)

    @pl.loop(1, groups)
    def _(d):
        p = lax.rem(place + d, groups)
        remote(
            gath.at[core, place], gath.at[core, place], main_ag, device(2 * p + core)
        ).start()

    wait_bytes(half.at[others], main_ag.at[1])
    back = remote(gath.at[core], gath.at[core], pair_ag, partner)
    back.start()
    back.wait_recv()

    left = gath[0].reshape(groups * piece, 128).astype(F32)
    right = gath[1].reshape(groups * piece, 128).astype(F32)
    full = right + pltpu.roll(right, 96, 1)
    s = jnp.concatenate([left[0:n1], right[0:n1, 0:64]], axis=1)
    gsum = full[0:n1, 64:65]
    triple_ref[...] = s * scale_ref[...] + gsum * offset_ref[...]
    stencil_out_ref[...] = full[0:n1, 72:81]
    outgoing_ref[...] = jnp.concatenate([left[n1:n2], right[n1:n2, 0:64]], axis=1)
    sharp_out_ref[...] = full[n1 : n1 + 1, 64:68]
    eye = lax.broadcasted_iota(jnp.int32, (channels, channels), 0) == lax.broadcasted_iota(
        jnp.int32, (channels, channels), 1
    )
    scaling_ref[...] = jnp.sum(jnp.where(eye, full[n1:n2, 72:73], 0.0), axis=0, keepdims=True)
    offset_out_ref[...] = jnp.sum(mixer_f * gsum, axis=0, keepdims=True)

    @pl.when(has_hi)
    def _():
        for copy in to_next():
            copy.wait_send()

    @pl.when(has_lo)
    def _():
        for copy in to_previous():
            copy.wait_send()

    @pl.when(owner)
    def _():
        wait_bytes(gram.at[pl.ds(0, owners - 1)], gram_rs.at[0])
        wait_bytes(gram_recv.at[rest], gram_ag.at[0])

    @pl.when(jnp.logical_not(owner))
    def _():
        wait_bytes(gram, gram_rs.at[0])

    swap.wait_send()
    wait_bytes(recv.at[others], main_rs.at[0])
    wait_bytes(half.at[others], main_ag.at[0])
    back.wait_send()


def local(
    block_feature_map, upstream_sensitivity, triple_mixer, spatial_stencil, outgoing_mixer,
    sharpness_factor, standardize_scaling, standardize_offset,
):
    _, channels, rows, width = block_feature_map.shape
    n_img = lax.axis_size("img")
    n_tile = lax.axis_size("tile")
    groups = n_img * n_tile // 2
    own = jnp.transpose(block_feature_map[0], (1, 0, 2))
    cot = jnp.transpose(upstream_sensitivity[0], (1, 0, 2))
    n1 = 3 * channels
    each = -(-channels // (n_tile * 8)) * 8
    owners = -(-channels // each)
    piece = -(-4 * channels // (groups * 16)) * 16

    shape = jax.ShapeDtypeStruct
    vmem = pltpu.VMEM
    pair_sem = pltpu.SemaphoreType.DMA((2,))
    out, triple, stencil, outgoing, sharp, scaling, offset = pl.pallas_call(
        functools.partial(kernel, n_img, n_tile),
        out_shape=(
            shape((rows, channels, width), BF16),
            shape((n1, channels), F32),
            shape((n1, 9), F32),
            shape((channels, channels), F32),
            shape((1, sharpness_factor.shape[0]), F32),
            shape((1, channels), F32),
            shape((1, channels), F32),
        ),
        in_specs=[VMEM] * 7 + [SMEM],
        out_specs=[VMEM] * 7,
        scratch_shapes=[
            vmem((3, channels, width), BF16),
            vmem((3, channels, width), BF16),
            vmem((rows + 4, n1, width), BF16),
            vmem((rows + 2, n1, width), BF16),
            vmem((rows + 2, channels, width), BF16),
            vmem((rows + 2, n1, width), BF16),
            vmem((rows, n1, width), BF16),
            vmem((5, channels, 256), F32),
            vmem((owners, each, 128), F32),
            vmem((n_tile, each, 128), F32),
            vmem((owners, each, 128), F32),
            vmem((channels, channels), BF16),
            vmem((channels, channels), BF16),
            vmem((channels, channels), BF16),
            vmem((channels, 128), F32),
            vmem((n1, 256), F32),
            vmem((4 * channels, 128), F32),
            vmem((2, groups, piece, 128), BF16),
            vmem((groups, piece, 128), BF16),
            vmem((groups, piece, 128), BF16),
            vmem((groups, piece, 128), BF16),
            vmem((2, groups, piece, 128), BF16),
        ]
        + [pair_sem] * 10,
        compiler_params=pltpu.CompilerParams(
            collective_id=0, has_side_effects=True, vmem_limit_bytes=LIMIT
        ),
        name="block",
    )(
        own, cot, triple_mixer, spatial_stencil.reshape(n1, 9), outgoing_mixer,
        standardize_scaling.reshape(1, channels), standardize_offset.reshape(1, channels),
        sharpness_factor,
    )
    return (
        jnp.transpose(out, (1, 0, 2))[None],
        triple,
        stencil.reshape(n1, 3, 3),
        outgoing,
        sharp[0],
        scaling[0],
        offset[0],
    )


def solution(mesh):
    rows = P("img", None, "tile", None)
    return jax.shard_map(
        local,
        mesh=mesh,
        in_specs=(rows, rows, P(), P(), P(), P(), P(), P()),
        out_specs=(rows, P(), P(), P(), P(), P(), P()),
        check_vma=False,
    )
```

time: 117 us -> 91.5 us (0.78)
  Pallas kernels: 93.6 us -> 77.1 us
  other arithmetic: 4.8 us -> 0 us
  starting transfers between devices: 3.67 us -> 0 us
    pallas_call x4 -> x1, Pallas kernels: 93.6 us -> 77.1 us  [local(): pl.pallas_call(functools.partial(kernel, n_img, n_tile), out_shape=(shape...]
    unnamed x20 -> x21, local copies, waits for them, and re-layouts: 3.36 us -> 7.94 us
    slice x11 -> x0, local copies, waits for them, and re-layouts: 3.95 us -> none  [the longest x1 1.54 us: all_reduce(): return out.reshape(n * each, 128)[:rows]]
    ppermute x2 -> x0, starting transfers between devices: 3.67 us -> none  [the longest x1 2.37 us: local(): lo = lax.ppermute(last, 'tile', up)]
    convert_element_type x2 -> x0, other arithmetic: 1.64 us -> none  [the longest x1 1.05 us: local(): red = all_reduce(red, ('img', 'tile'), 16, 2).astype(F32)]
    pad x1 -> x0, local copies, waits for them, and re-layouts: 1.56 us -> none  [all_reduce(): x = jnp.pad(x, ((0, each * n - rows), (0, 0)))]
    reduce_sum x1 -> x0, other arithmetic: 1.49 us -> none  [local(): jnp.sum(mixer * gsum, axis=0)]
    reshape x5 -> x3, local copies, waits for them, and re-layouts: 3.05 us -> 2.37 us  [the longest x2 1.72 us: local(): spatial_stencil.reshape(n1, 9)]
  transfers between devices with their start and end apart: 2 -> 0, of which waited for: 1 -> 0; matrix products, arithmetic and copies ran while one was open for 3% -> 0% of each run, Pallas kernels for 0% -> 0%
where the time goes in v2:
time: 91.5 us; the launch traced here: 90.9 us
  Pallas kernels  77.1 us (84%)
  local copies, waits for them, and re-layouts  13.1 us (14%)
    pallas_call x1, Pallas kernels, local(): pl.pallas_call(functools.partial(kernel, n_img, n_tile), out_shape=(shape...  77.1 us
    unnamed x21, local copies, waits for them, and re-layouts  7.94 us
    transpose x1, local copies, waits for them, and re-layouts, local(): cot = jnp.transpose(upstream_sensitivity[0], (1, 0, 2))  2.63 us

profile of v2, /device:TPU:0, one launch (start us, length us, event | category | flops | bytes accessed | tf_op | source)
XLA Modules:
  0.0 90.9 jit_solution(5250638604186012139)
XLA Ops:
  0.6 0.0 copy-start
  0.6 0.8 reshape.26
  1.5 0.9 copy.25.stencil_ref
  2.4 1.8 %copy.24.mixer_ref = bf16[576,192]{1,0:T(8,128)(2,1)} copy(bf16[576,192]{0,1:T(8,128)(2,1)} %param.10) | data formatting | bytes 442368 | tf_op args[2]
  4.2 0.0 copy-done
  4.2 2.6 %copy_bitcast_fusion = (bf16[8,192,256]{2,1,0:T(8,128)(2,1)}, bf16[8,192,256]{2,1,0:T(8,128)(2,1)}) fusion(bf16[1,192,8,256]{3,2,1,0:T(8,128)(2,1)S(1)} %copy-done, bf16[1,192,8,256]{3,2,1,0:T(8,128)(2,1)} %param.8), kind=kLoop, calls=%fused_computation | loop fusion | bytes 3145728 | tf_op jit(solution)/shard_map/transpose | solution.py:470
  6.8 77.1 %block.1 = (bf16[8,192,256]{2,1,0:T(8,128)(2,1)}, f32[576,192]{1,0:T(8,128)}, f32[576,9]{1,0:T(8,128)}, f32[192,192]{1,0:T(8,128)}, f32[1,4]{1,0:T(1,128)}, /*index=5*/f32[1,192]{1,0:T(1,128)}, f32[1,192]{1,0:T(1,128)}) custom-call(bf16[8,192,256]{2,1,0:T(8,128)(2,1)} %get-tuple-element.36.own_ref, bf16[8,192,256]{2,1,0:T(8,128)(2,1)} %get-tuple-element.35.cot_ref, ...), custom_call_target="tpu_custom_call" | custom-call | tf_op jit(solution)/shard_map/block/pallas_call | solution.py:479
  83.9 0.0 copy-start.2
  83.9 0.0 copy-start.1
  84.0 2.5 %copy.27 = bf16[1,192,8,256]{3,2,1,0:T(8,128)(2,1)} copy(bf16[1,192,8,256]{3,1,2,0:T(8,128)(2,1)} %bitcast.20) | data formatting | bytes 1572864
  86.5 0.0 copy-done.2
  86.5 0.1 copy.26
  86.6 0.7 reshape.29
  87.3 0.0 copy-done.1
  87.3 0.0 copy-start.3
  87.3 1.0 %copy.28 = f32[576,192]{0,1:T(8,128)} copy(f32[576,192]{1,0:T(8,128)S(1)} %copy-done.1) | data formatting | bytes 884736
  88.3 0.0 copy-done.3
  88.3 0.0 copy-start.6
  88.3 0.7 copy.35
  89.0 0.0 copy-done.6
  89.0 0.0 copy-start.5
  89.0 0.5 copy.36
  89.5 0.2 copy-done.5
  89.6 0.0 copy-start.4
  89.6 0.6 copy.37
  90.2 0.1 copy-done.4
  90.3 0.6 copy.38
Async XLA Ops:
  0.6 3.5 %copy-start = (bf16[1,192,8,256]{3,2,1,0:T(8,128)(2,1)S(1)}, bf16[1,192,8,256]{3,2,1,0:T(8,128)(2,1)}, u32[]{:S(2)}) copy-start(bf16[1,192,8,256]{3,2,1,0:T(8,128)(2,1)} %param.9) | copy-start | bytes 2359300
  83.9 2.5 %copy-start.2 = (f32[576,9]{1,0:T(8,128)S(1)}, f32[576,9]{1,0:T(8,128)}, u32[]{:S(2)}) copy-start(f32[576,9]{1,0:T(8,128)} %get-tuple-element.16) | copy-start | bytes 62212
  83.9 3.3 %copy-start.1 = (f32[576,192]{1,0:T(8,128)S(1)}, f32[576,192]{1,0:T(8,128)}, u32[]{:S(2)}) copy-start(f32[576,192]{1,0:T(8,128)} %get-tuple-element.29) | copy-start | bytes 1327108
  87.3 1.0 %copy-start.3 = (f32[192,192]{1,0:T(8,128)S(1)}, f32[192,192]{1,0:T(8,128)}, u32[]{:S(2)}) copy-start(f32[192,192]{1,0:T(8,128)} %get-tuple-element.47) | copy-start | bytes 442372
  88.3 0.7 copy-start.6
  89.0 0.7 copy-start.5
  89.6 0.7 copy-start.4

commit v3 on v2

--- a/solution.py
+++ b/solution.py
@@ -53,13 +53,13 @@
 
 def kernel(
     n_img, n_tile,
-    own_ref, cot_ref, mixer_ref, stencil_ref, out_mixer_ref, scale_ref, offset_ref, sharp_ref,
+    own_in, cot_in, mixer_t, stencil_in, out_mixer_ref, scale_ref, offset_ref, sharp_ref,
     out_ref, triple_ref, stencil_out_ref, outgoing_ref, sharp_out_ref, scaling_ref, offset_out_ref,
-    lo, hi, proj, mixed, ga, gm, gp, acc, gram, gram_recv, gram_all, gg_ref, ggt_ref, at_ref, coef,
+    own32, cot32, own_ref, cot_ref, mixer_ref, om_t, stencil_ref, lo, hi, proj, mixed, ga, gm, gp, acc, gram, gram_recv, gram_all, gg_ref, ggt_ref, at_ref, coef,
     sacc, extra, red, pair, half, recv, gath,
-    lo_x, lo_c, hi_x, hi_c, gram_rs, gram_ag, pair_rs, main_rs, main_ag, pair_ag,
+    lo_x, lo_c, hi_x, hi_c, gram_rs, gram_ag, pair_rs, main_rs, pair_ag, ag_send, ag_recv,
 ):
-    rows, channels, width = own_ref.shape
+    channels, rows, width = own_in.shape
     heads = channels // 48
     img = lax.axis_index("img")
     tile = lax.axis_index("tile")
@@ -78,6 +78,29 @@
             device_id_type=pl.DeviceIdType.MESH,
         )
 
+    def line_of(ref, r):
+        return jnp.concatenate(
+            [ref[pl.ds(c * channels * rows + r, channels, stride=rows), :] for c in range(width // 128)],
+            axis=1,
+        )
+
+    for c in range(width // 128):
+        part = pl.ds(c * channels * rows, channels * rows)
+        cols = slice(128 * c, 128 * c + 128)
+        own32[part, :] = own_in[:, :, cols].astype(F32).reshape(channels * rows, 128)
+        cot32[part, :] = cot_in[:, :, cols].astype(F32).reshape(channels * rows, 128)
+    for r in range(rows):
+        own_ref[r] = line_of(own32, r).astype(BF16)
+        cot_ref[r] = line_of(cot32, r).astype(BF16)
+
+    mixer_ref[...] = mixer_t[...].T
+    om_t[...] = out_mixer_ref[...].T
+    taps = jnp.concatenate(
+        [stencil_in[t // 3, t % 3 : t % 3 + 1, :] for t in range(9)]
+        + [jnp.zeros((119, 3 * channels), F32)], axis=0,
+    )
+    stencil_ref[...] = taps.T
+
     pl.semaphore_wait(barrier, n - 1)
 
     def to_next():
@@ -109,18 +132,16 @@
 
     scale = column(scale_ref[...])
     offset = column(offset_ref[...])
-    mixer = mixer_ref[...]
-    out_mixer = out_mixer_ref[...]
 
     def project(x):
         standard, _ = standardized(x)
         normed = (standard * scale + offset).astype(BF16)
-        return dot(mixer, normed).astype(BF16)
+        return dot(mixer_ref[...], normed).astype(BF16)
 
     @pl.loop(0, rows, unroll=2)
     def _(r):
         proj[r + 2] = project(own_ref[r])
-        ga[r + 1] = dot(out_mixer, cot_ref[r], TN).astype(BF16)
+        ga[r + 1] = dot(om_t[...], cot_ref[r]).astype(BF16)
 
     @pl.when(has_lo)
     def _():
@@ -128,7 +149,7 @@
             copy.wait_recv()
         for i in range(2):
             proj[i] = project(lo[i])
-        ga[0] = dot(out_mixer, lo[2], TN).astype(BF16)
+        ga[0] = dot(om_t[...], lo[2]).astype(BF16)
 
     @pl.when(jnp.logical_not(has_lo))
     def _():
@@ -141,7 +162,7 @@
             copy.wait_recv()
         for i in range(2):
             proj[rows + 2 + i] = project(hi[i])
-        ga[rows + 1] = dot(out_mixer, hi[2], TN).astype(BF16)
+        ga[rows + 1] = dot(om_t[...], hi[2]).astype(BF16)
 
     @pl.when(jnp.logical_not(has_hi))
     def _():
@@ -312,16 +333,16 @@
     @pl.loop(0, 3 * channels // group)
     def _(g):
         at = pl.ds(pl.multiple_of(g * group, group), group)
-        tap = [jnp.zeros((group, width), F32) for _ in range(9)]
+        tap = [jnp.zeros((group, 128), F32) for _ in range(9)]
         line = [proj[1 + i, at, :].astype(F32) for i in range(2)]
         for r in range(rows):
             line.append(proj[r + 3, at, :].astype(F32))
             g_mid = gm[r + 1, at, :].astype(F32)
             right, left = shifted(g_mid, lanes)
             for a in range(3):
-                tap[3 * a] += line[r + a] * left
-                tap[3 * a + 1] += line[r + a] * g_mid
-                tap[3 * a + 2] += line[r + a] * right
+                for b, side in enumerate((left, g_mid, right)):
+                    for c in range(0, width, 128):
+                        tap[3 * a + b] += line[r + a][:, c : c + 128] * side[:, c : c + 128]
         total = jnp.zeros((group, 128), F32)
         for t in range(9):
             s = jnp.sum(tap[t], axis=1, keepdims=True)
@@ -368,8 +389,22 @@
     partner = {"img": img, "tile": tile + 1 - 2 * core}
     others = pl.ds(0, groups - 1)
 
+    def feature_rows(first_row, last_row):
+        @pl.loop(first_row, last_row, unroll=2)
+        def _(r):
+            standard, inverse = standardized(own_ref[r])
+            scaled = dot(mixer_t[...], gp[r]) * scale
+            first = jnp.mean(scaled, axis=0, keepdims=True)
+            second = jnp.mean(scaled * standard, axis=0, keepdims=True)
+            adjoint = cot_ref[r].astype(F32) + (scaled - first - standard * second) * inverse
+            for c in range(width // 128):
+                own32[pl.ds(c * channels * rows + r, channels, stride=rows), :] = adjoint[
+                    :, 128 * c : 128 * c + 128
+                ]
+
     swap = remote(red.at[1 - core], pair, pair_rs, partner)
     swap.start()
+    feature_rows(0, 2)
     swap.wait_recv()
 
     def rounded(x):
@@ -388,16 +423,10 @@
 
     recv[place] = half[place]
 
-    @pl.loop(0, rows, unroll=2)
-    def _(r):
-        standard, inverse = standardized(own_ref[r])
-        scaled = dot(mixer, gp[r], TN) * scale
-        first = jnp.mean(scaled, axis=0, keepdims=True)
-        second = jnp.mean(scaled * standard, axis=0, keepdims=True)
-        out_ref[r] = (
-            cot_ref[r].astype(F32) + (scaled - first - standard * second) * inverse
-        ).astype(BF16)
-
+    feature_rows(2, rows)
+    for c in range(width // 128):
+        part = own32[pl.ds(c * channels * rows, channels * rows), :]
+        out_ref[:, :, 128 * c : 128 * c + 128] = part.reshape(channels, rows, 128).astype(BF16)
     wait_bytes(recv.at[others], main_rs.at[1])
 
     def add(i, total):
@@ -409,14 +438,21 @@
     @pl.loop(1, groups)
     def _(d):
         p = lax.rem(place + d, groups)
-        remote(
-            gath.at[core, place], gath.at[core, place], main_ag, device(2 * p + core)
+        pltpu.make_async_remote_copy(
+            src_ref=gath.at[core, place], dst_ref=gath.at[core, place], send_sem=ag_send,
+            recv_sem=ag_recv.at[place], device_id=device(2 * p + core),
+            device_id_type=pl.DeviceIdType.MESH,
         ).start()
 
-    wait_bytes(half.at[others], main_ag.at[1])
-    back = remote(gath.at[core], gath.at[core], pair_ag, partner)
-    back.start()
-    back.wait_recv()
+    remote(gath.at[core, place], gath.at[core, place], pair_ag, partner).start()
+
+    @pl.loop(1, groups)
+    def _(d):
+        p = lax.rem(place + groups - d, groups)
+        wait_bytes(gath.at[core, p], ag_recv.at[p])
+        remote(gath.at[core, p], gath.at[core, p], pair_ag, partner).start()
+
+    wait_bytes(gath.at[1 - core], pair_ag.at[1])
 
     left = gath[0].reshape(groups * piece, 128).astype(F32)
     right = gath[1].reshape(groups * piece, 128).astype(F32)
@@ -454,8 +490,8 @@
 
     swap.wait_send()
     wait_bytes(recv.at[others], main_rs.at[0])
-    wait_bytes(half.at[others], main_ag.at[0])
-    back.wait_send()
+    wait_bytes(half.at[others], ag_send)
+    wait_bytes(gath.at[core], pair_ag.at[0])
 
 
 def local(
@@ -466,8 +502,6 @@
     n_img = lax.axis_size("img")
     n_tile = lax.axis_size("tile")
     groups = n_img * n_tile // 2
-    own = jnp.transpose(block_feature_map[0], (1, 0, 2))
-    cot = jnp.transpose(upstream_sensitivity[0], (1, 0, 2))
     n1 = 3 * channels
     each = -(-channels // (n_tile * 8)) * 8
     owners = -(-channels // each)
@@ -479,7 +513,7 @@
     out, triple, stencil, outgoing, sharp, scaling, offset = pl.pallas_call(
         functools.partial(kernel, n_img, n_tile),
         out_shape=(
-            shape((rows, channels, width), BF16),
+            shape((channels, rows, width), BF16),
             shape((n1, channels), F32),
             shape((n1, 9), F32),
             shape((channels, channels), F32),
@@ -490,6 +524,13 @@
         in_specs=[VMEM] * 7 + [SMEM],
         out_specs=[VMEM] * 7,
         scratch_shapes=[
+            vmem((channels * rows * width // 128, 128), F32),
+            vmem((channels * rows * width // 128, 128), F32),
+            vmem((rows, channels, width), BF16),
+            vmem((rows, channels, width), BF16),
+            vmem((n1, channels), BF16),
+            vmem((channels, channels), BF16),
+            vmem((n1, 128), F32),
             vmem((3, channels, width), BF16),
             vmem((3, channels, width), BF16),
             vmem((rows + 4, n1, width), BF16),
@@ -513,18 +554,20 @@
             vmem((groups, piece, 128), BF16),
             vmem((2, groups, piece, 128), BF16),
         ]
-        + [pair_sem] * 10,
+        + [pair_sem] * 9
+        + [pltpu.SemaphoreType.DMA, pltpu.SemaphoreType.DMA((groups,))],
         compiler_params=pltpu.CompilerParams(
             collective_id=0, has_side_effects=True, vmem_limit_bytes=LIMIT
         ),
         name="block",
     )(
-        own, cot, triple_mixer, spatial_stencil.reshape(n1, 9), outgoing_mixer,
+        block_feature_map[0], upstream_sensitivity[0], triple_mixer.T,
+        jnp.transpose(spatial_stencil, (1, 2, 0)), outgoing_mixer,
         standardize_scaling.reshape(1, channels), standardize_offset.reshape(1, channels),
         sharpness_factor,
     )
     return (
-        jnp.transpose(out, (1, 0, 2))[None],
+        out[None],
         triple,
         stencil.reshape(n1, 3, 3),
         outgoing,

time: 91.5 us -> 85.4 us (0.933)
  local copies, waits for them, and re-layouts: 13.1 us -> 7.58 us
    transpose x1 -> x0, local copies, waits for them, and re-layouts: 2.63 us -> none  [local(): cot = jnp.transpose(upstream_sensitivity[0], (1, 0, 2))]
    unnamed x21 -> x16, local copies, waits for them, and re-layouts: 7.94 us -> 5.76 us
    reshape x2 -> x0, local copies, waits for them, and re-layouts: 1.72 us -> none  [local(): spatial_stencil.reshape(n1, 9)]
    pallas_call x1, local copies, waits for them, and re-layouts: 0.13 us -> 1.16 us  [local(): pl.pallas_call(functools.partial(kernel, n_img, n_tile), out_shape=(shape...]
where the time goes in v3:
time: 85.4 us; the launch traced here: 84.9 us
  Pallas kernels  76.7 us (90%)
  local copies, waits for them, and re-layouts  7.58 us (9%)
    pallas_call x1, Pallas kernels, local(): pl.pallas_call(functools.partial(kernel, n_img, n_tile), out_shape=(shape...  76.7 us
    unnamed x16, local copies, waits for them, and re-layouts  5.76 us

profile of v3, /device:TPU:0, one launch (start us, length us, event | category | flops | bytes accessed | tf_op | source)
XLA Modules:
  0.0 84.9 jit_solution(4427799916032866208)
XLA Ops:
  0.6 76.7 %block.1 = (bf16[192,8,256]{2,1,0:T(8,128)(2,1)}, f32[576,192]{1,0:T(8,128)}, f32[576,9]{1,0:T(8,128)}, f32[192,192]{1,0:T(8,128)}, f32[1,4]{1,0:T(1,128)}, /*index=5*/f32[1,192]{1,0:T(1,128)}, f32[1,192]{1,0:T(1,128)}) custom-call(bf16[192,8,256]{2,1,0:T(8,128)(2,1)} %bitcast.12, bf16[192,8,256]{2,1,0:T(8,128)(2,1)} %bitcast.13, bf16[192,576]{1,0:T(8,128)(2,1)} %bitcast.15, ...), custom_call_target="tpu_custom_call" | custom-call | tf_op jit(solution)/shard_map/block/pallas_call | solution.py:513
  77.3 0.0 copy-start
  77.3 1.2 %copy.17 = f32[576,9]{0,1:T(8,128)S(1)} copy(f32[576,9]{1,0:T(8,128)} %get-tuple-element.16) | data formatting | bytes 41472 | tf_op jit(solution)/shard_map/block/pallas_call | solution.py:513
  78.5 0.7 reshape.25
  79.1 2.1 %copy.18 = f32[576,192]{0,1:T(8,128)} copy(f32[576,192]{1,0:T(8,128)} %get-tuple-element.29) | data formatting | bytes 884736
  81.2 0.0 copy-done
  81.2 0.0 copy-start.1
  81.2 0.9 %copy.24 = bf16[1,192,8,256]{3,2,1,0:T(8,128)(2,1)} copy(bf16[1,192,8,256]{3,2,1,0:T(8,128)(2,1)S(1)} %bitcast.14) | data formatting | bytes 1572864
  82.1 0.2 copy-done.1
  82.3 0.0 copy-start.4
  82.3 0.7 copy.25
  83.0 0.0 copy-done.4
  83.0 0.0 copy-start.3
  83.0 0.5 copy.26
  83.5 0.2 copy-done.3
  83.7 0.0 copy-start.2
  83.7 0.6 copy.27
  84.2 0.1 copy-done.2
  84.3 0.6 copy.28
Async XLA Ops:
  77.3 3.9 %copy-start = (bf16[192,8,256]{2,1,0:T(8,128)(2,1)S(1)}, bf16[192,8,256]{2,1,0:T(8,128)(2,1)}, u32[]{:S(2)}) copy-start(bf16[192,8,256]{2,1,0:T(8,128)(2,1)} %get-tuple-element.14) | copy-start | bytes 2359300
  81.2 1.1 %copy-start.1 = (f32[192,192]{1,0:T(8,128)S(1)}, f32[192,192]{1,0:T(8,128)}, u32[]{:S(2)}) copy-start(f32[192,192]{1,0:T(8,128)} %get-tuple-element.45) | copy-start | bytes 442372
  82.3 0.7 copy-start.4
  83.0 0.7 copy-start.3
  83.7 0.7 copy-start.2

commit v4 on v3

--- a/solution.py
+++ b/solution.py
@@ -54,8 +54,8 @@
 def kernel(
     n_img, n_tile,
     own_in, cot_in, mixer_t, stencil_in, out_mixer_ref, scale_ref, offset_ref, sharp_ref,
-    out_ref, triple_ref, stencil_out_ref, outgoing_ref, sharp_out_ref, scaling_ref, offset_out_ref,
-    own32, cot32, own_ref, cot_ref, mixer_ref, om_t, stencil_ref, lo, hi, proj, mixed, ga, gm, gp, acc, gram, gram_recv, gram_all, gg_ref, ggt_ref, at_ref, coef,
+    out_ref, gath_out,
+    own32, cot32, std32, ext, inv, own_ref, cot_ref, mixer_ref, om_t, stencil_ref, lo, hi, proj, mixed, ga, gm, gp, acc, gram, gram_recv, gram_all, gg_ref, ggt_ref, at_ref, coef,
     sacc, extra, red, pair, half, recv, gath,
     lo_x, lo_c, hi_x, hi_c, gram_rs, gram_ag, pair_rs, main_rs, pair_ag, ag_send, ag_recv,
 ):
@@ -140,16 +140,19 @@
 
     @pl.loop(0, rows, unroll=2)
     def _(r):
-        proj[r + 2] = project(own_ref[r])
+        standard, inverse = standardized(own_ref[r])
+        std32[r] = standard
+        inv[r] = inverse
+        ext[r, 0:channels, :] = standard.astype(BF16)
+        ext[r, channels:256, :] = jnp.ones((256 - channels, width), BF16)
+        normed = (standard * scale + offset).astype(BF16)
+        proj[r + 2] = dot(mixer_ref[...], normed).astype(BF16)
         ga[r + 1] = dot(om_t[...], cot_ref[r]).astype(BF16)
 
     @pl.when(has_lo)
     def _():
-        for copy in to_next():
-            copy.wait_recv()
-        for i in range(2):
-            proj[i] = project(lo[i])
-        ga[0] = dot(om_t[...], lo[2]).astype(BF16)
+        to_next()[0].wait_recv()
+        proj[1] = project(lo[1])
 
     @pl.when(jnp.logical_not(has_lo))
     def _():
@@ -158,11 +161,8 @@
 
     @pl.when(has_hi)
     def _():
-        for copy in to_previous():
-            copy.wait_recv()
-        for i in range(2):
-            proj[rows + 2 + i] = project(hi[i])
-        ga[rows + 1] = dot(om_t[...], hi[2]).astype(BF16)
+        to_previous()[0].wait_recv()
+        proj[rows + 2] = project(hi[0])
 
     @pl.when(jnp.logical_not(has_hi))
     def _():
@@ -172,20 +172,22 @@
     group = 16
     lanes = lax.broadcasted_iota(jnp.int32, (group, width), 1)
 
-    @pl.loop(0, 3 * channels // group)
-    def _(g):
-        at = pl.ds(pl.multiple_of(g * group, group), group)
-        weights = stencil_ref[at, :]
-        w = [jnp.broadcast_to(weights[:, t : t + 1], (group, width)) for t in range(9)]
-        line = [proj[i, at, :].astype(F32) for i in range(2)]
-        for r in range(rows + 2):
-            line.append(proj[r + 2, at, :].astype(F32))
-            sums = [
-                w[b] * line[r] + w[3 + b] * line[r + 1] + w[6 + b] * line[r + 2] for b in range(3)
-            ]
-            right = jnp.where(lanes == 0, 0.0, pltpu.roll(sums[0], 1, 1))
-            left = jnp.where(lanes == width - 1, 0.0, pltpu.roll(sums[2], width - 1, 1))
-            mixed[r, at, :] = (sums[1] + right + left).astype(BF16)
+    def mix(strips):
+        @pl.loop(0, 3 * channels // group)
+        def _(g):
+            at = pl.ds(pl.multiple_of(g * group, group), group)
+            weights = stencil_ref[at, :]
+            w = [jnp.broadcast_to(weights[:, t : t + 1], (group, width)) for t in range(9)]
+            for first_row, last_row in strips:
+                line = [proj[first_row + i, at, :].astype(F32) for i in range(2)]
+                for r in range(first_row, last_row):
+                    line = line[-2:] + [proj[r + 2, at, :].astype(F32)]
+                    sums = [w[b] * line[0] + w[3 + b] * line[1] + w[6 + b] * line[2] for b in range(3)]
+                    right = jnp.where(lanes == 0, 0.0, pltpu.roll(sums[0], 1, 1))
+                    left = jnp.where(lanes == width - 1, 0.0, pltpu.roll(sums[2], width - 1, 1))
+                    mixed[r, at, :] = (sums[1] + right + left).astype(BF16)
+
+    mix([(1, rows + 1)])
 
     acc[...] = jnp.zeros_like(acc)
 
@@ -196,7 +198,6 @@
         v = mixed[r + 1, 2 * channels : 3 * channels, :]
         acc[0, :, 0:channels] += dot(q, k, NT)
         acc[1, :, 0:channels] += dot(ga[r + 1], v, NT)
-        acc[2, :, 0:channels] += dot(cot_ref[r], v, NT)
         qf = q.astype(F32)
         kf = k.astype(F32)
         acc[3] += qf * qf
@@ -232,6 +233,20 @@
         def _():
             remote(gram.at[p], gram_recv.at[tile], gram_rs, {"img": img, "tile": p}).start()
 
+    @pl.when(has_lo)
+    def _():
+        to_next()[1].wait_recv()
+        proj[0] = project(lo[0])
+        ga[0] = dot(om_t[...], lo[2]).astype(BF16)
+
+    @pl.when(has_hi)
+    def _():
+        to_previous()[1].wait_recv()
+        proj[rows + 3] = project(hi[1])
+        ga[rows + 1] = dot(om_t[...], hi[2]).astype(BF16)
+
+    mix([(0, 1), (rows + 1, rows + 2)])
+
     @pl.when(owner)
     def _():
         gram_recv[tile] = gram[tile]
@@ -252,6 +267,11 @@
     at_ref[...] = jnp.zeros_like(at_ref)
     extra[...] = jnp.zeros_like(extra)
     sacc[...] = jnp.zeros_like(sacc)
+
+    @pl.loop(0, rows, unroll=2)
+    def _(r):
+        acc[2, :, 0:channels] += dot(cot_ref[r], mixed[r + 1, 2 * channels : 3 * channels, :], NT)
+
 
     @pl.when(owner)
     def _():
@@ -351,9 +371,7 @@
 
     @pl.loop(0, rows, unroll=2)
     def _(r):
-        standard, _ = standardized(own_ref[r])
-        ext = jnp.concatenate([standard.astype(BF16), jnp.ones((64, width), BF16)], axis=0)
-        sacc[...] += dot(gp[r], ext, NT)
+        sacc[...] += dot(gp[r], ext[r], NT)
 
     n1 = 3 * channels
     n2 = 4 * channels
@@ -392,7 +410,8 @@
     def feature_rows(first_row, last_row):
         @pl.loop(first_row, last_row, unroll=2)
         def _(r):
-            standard, inverse = standardized(own_ref[r])
+            standard = std32[r]
+            inverse = inv[r]
             scaled = dot(mixer_t[...], gp[r]) * scale
             first = jnp.mean(scaled, axis=0, keepdims=True)
             second = jnp.mean(scaled * standard, axis=0, keepdims=True)
@@ -423,10 +442,7 @@
 
     recv[place] = half[place]
 
-    feature_rows(2, rows)
-    for c in range(width // 128):
-        part = own32[pl.ds(c * channels * rows, channels * rows), :]
-        out_ref[:, :, 128 * c : 128 * c + 128] = part.reshape(channels, rows, 128).astype(BF16)
+    feature_rows(2, 6)
     wait_bytes(recv.at[others], main_rs.at[1])
 
     def add(i, total):
@@ -445,6 +461,10 @@
         ).start()
 
     remote(gath.at[core, place], gath.at[core, place], pair_ag, partner).start()
+    feature_rows(6, rows)
+    for c in range(width // 128):
+        part = own32[pl.ds(c * channels * rows, channels * rows), :]
+        out_ref[:, :, 128 * c : 128 * c + 128] = part.reshape(channels, rows, 128).astype(BF16)
 
     @pl.loop(1, groups)
     def _(d):
@@ -454,20 +474,7 @@
 
     wait_bytes(gath.at[1 - core], pair_ag.at[1])
 
-    left = gath[0].reshape(groups * piece, 128).astype(F32)
-    right = gath[1].reshape(groups * piece, 128).astype(F32)
-    full = right + pltpu.roll(right, 96, 1)
-    s = jnp.concatenate([left[0:n1], right[0:n1, 0:64]], axis=1)
-    gsum = full[0:n1, 64:65]
-    triple_ref[...] = s * scale_ref[...] + gsum * offset_ref[...]
-    stencil_out_ref[...] = full[0:n1, 72:81]
-    outgoing_ref[...] = jnp.concatenate([left[n1:n2], right[n1:n2, 0:64]], axis=1)
-    sharp_out_ref[...] = full[n1 : n1 + 1, 64:68]
-    eye = lax.broadcasted_iota(jnp.int32, (channels, channels), 0) == lax.broadcasted_iota(
-        jnp.int32, (channels, channels), 1
-    )
-    scaling_ref[...] = jnp.sum(jnp.where(eye, full[n1:n2, 72:73], 0.0), axis=0, keepdims=True)
-    offset_out_ref[...] = jnp.sum(mixer_f * gsum, axis=0, keepdims=True)
+    gath_out[...] = gath[...]
 
     @pl.when(has_hi)
     def _():
@@ -492,6 +499,31 @@
     wait_bytes(recv.at[others], main_rs.at[0])
     wait_bytes(half.at[others], ag_send)
     wait_bytes(gath.at[core], pair_ag.at[0])
+
+
+def finish_kernel(
+    adjoint_ref, gath_ref, mixer_t, scale_ref, offset_ref,
+    out_ref, triple_ref, stencil_ref, outgoing_ref, sharp_ref, scaling_ref, offset_out_ref, sem,
+):
+    move = pltpu.make_async_copy(adjoint_ref, out_ref, sem)
+    move.start()
+    channels, n1 = mixer_t.shape
+    n2 = n1 + channels
+    left = gath_ref[0].reshape(-1, 128).astype(F32)
+    right = gath_ref[1].reshape(-1, 128).astype(F32)
+    full = right + pltpu.roll(right, 96, 1)
+    s = jnp.concatenate([left[0:n1], right[0:n1, 0:64]], axis=1)
+    gsum = full[0:n1, 64:65]
+    triple_ref[...] = (s * scale_ref[...] + gsum * offset_ref[...]).T
+    turned = full[0:n1].T
+    for t in range(9):
+        stencil_ref[t // 3, t % 3 : t % 3 + 1, :] = turned[72 + t : 73 + t, :]
+    outgoing_ref[...] = jnp.concatenate([left[n1:n2], right[n1:n2, 0:64]], axis=1)
+    sharp_ref[...] = full[n1 : n1 + 1, 64:68]
+    scaling_ref[...] = full[n1:n2].T[72:73, :]
+    mixer = mixer_t[...].T.astype(F32)
+    offset_out_ref[...] = jnp.sum(mixer * gsum, axis=0, keepdims=True)
+    move.wait()
 
 
 def local(
@@ -510,22 +542,23 @@
     shape = jax.ShapeDtypeStruct
     vmem = pltpu.VMEM
     pair_sem = pltpu.SemaphoreType.DMA((2,))
-    out, triple, stencil, outgoing, sharp, scaling, offset = pl.pallas_call(
+    mixer_t = triple_mixer.T
+    scale_row = standardize_scaling.reshape(1, channels)
+    offset_row = standardize_offset.reshape(1, channels)
+    adjoint, gathered = pl.pallas_call(
         functools.partial(kernel, n_img, n_tile),
         out_shape=(
             shape((channels, rows, width), BF16),
-            shape((n1, channels), F32),
-            shape((n1, 9), F32),
-            shape((channels, channels), F32),
-            shape((1, sharpness_factor.shape[0]), F32),
-            shape((1, channels), F32),
-            shape((1, channels), F32),
+            shape((2, groups, piece, 128), BF16),
         ),
         in_specs=[VMEM] * 7 + [SMEM],
-        out_specs=[VMEM] * 7,
+        out_specs=[VMEM] * 2,
         scratch_shapes=[
             vmem((channels * rows * width // 128, 128), F32),
             vmem((channels * rows * width // 128, 128), F32),
+            vmem((rows, channels, width), F32),
+            vmem((rows, 256, width), BF16),
+            vmem((rows, 1, width), F32),
             vmem((rows, channels, width), BF16),
             vmem((rows, channels, width), BF16),
             vmem((n1, channels), BF16),
@@ -561,15 +594,32 @@
         ),
         name="block",
     )(
-        block_feature_map[0], upstream_sensitivity[0], triple_mixer.T,
-        jnp.transpose(spatial_stencil, (1, 2, 0)), outgoing_mixer,
-        standardize_scaling.reshape(1, channels), standardize_offset.reshape(1, channels),
+        block_feature_map[0], upstream_sensitivity[0], mixer_t,
+        jnp.transpose(spatial_stencil, (1, 2, 0)), outgoing_mixer, scale_row, offset_row,
         sharpness_factor,
     )
+    anywhere = pl.BlockSpec(memory_space=pl.ANY)
+    out, triple, stencil, outgoing, sharp, scaling, offset = pl.pallas_call(
+        finish_kernel,
+        out_shape=(
+            shape((channels, rows, width), BF16),
+            shape((channels, n1), F32),
+            shape((3, 3, n1), F32),
+            shape((channels, channels), F32),
+            shape((1, sharpness_factor.shape[0]), F32),
+            shape((1, channels), F32),
+            shape((1, channels), F32),
+        ),
+        in_specs=[anywhere] + [VMEM] * 4,
+        out_specs=[anywhere] + [VMEM] * 6,
+        scratch_shapes=[pltpu.SemaphoreType.DMA],
+        compiler_params=pltpu.CompilerParams(vmem_limit_bytes=32 * 1024 * 1024),
+        name="finish",
+    )(adjoint, gathered, mixer_t, scale_row, offset_row)
     return (
         out[None],
-        triple,
-        stencil.reshape(n1, 3, 3),
+        triple.T,
+        jnp.transpose(stencil, (2, 0, 1)),
         outgoing,
         sharp[0],
         scaling[0],

time: 85.4 us -> 82.7 us (0.968)
  local copies, waits for them, and re-layouts: 7.58 us -> 2.79 us
  Pallas kernels: 76.7 us -> 78.9 us
    unnamed x16 -> x10, local copies, waits for them, and re-layouts: 5.76 us -> 2.79 us
    pallas_call x0 -> x1, Pallas kernels: none -> 1.76 us  [local(): pl.pallas_call(finish_kernel, out_shape=(shape((channels, rows, width), B...]
    pallas_call x1 -> x0, local copies, waits for them, and re-layouts: 1.16 us -> none  [local(): pl.pallas_call(functools.partial(kernel, n_img, n_tile), out_shape=(shape...]
where the time goes in v4:
time: 82.7 us; the launch traced here: 82.4 us
  Pallas kernels  78.9 us (95%)
  local copies, waits for them, and re-layouts  2.79 us (3%)
    pallas_call x1, Pallas kernels, local(): pl.pallas_call(functools.partial(kernel, n_img, n_tile), out_shape=(shape...  77.2 us
    unnamed x10, local copies, waits for them, and re-layouts  2.79 us
    pallas_call x1, Pallas kernels, local(): pl.pallas_call(finish_kernel, out_shape=(shape((channels, rows, width), B...  1.76 us

profile of v4, /device:TPU:0, one launch (start us, length us, event | category | flops | bytes accessed | tf_op | source)
XLA Modules:
  0.0 82.4 jit_solution(3737171905402121163)
XLA Ops:
  0.6 0.0 copy-start
  0.6 0.0 copy-start.4
  0.7 77.2 %block.1 = (bf16[192,8,256]{2,1,0:T(8,128)(2,1)}, bf16[2,16,48,128]{3,2,1,0:T(8,128)(2,1)}) custom-call(bf16[192,8,256]{2,1,0:T(8,128)(2,1)} %bitcast.18, bf16[192,8,256]{2,1,0:T(8,128)(2,1)} %bitcast.19, bf16[192,576]{1,0:T(8,128)(2,1)} %bitcast.12, f32[3,3,576]{2,1,0:T(4,128)} %bitcast.20, bf16[192,192]{1,0:T(8,128)(2,1)} %out_mixer_ref.1, ...), custom_call_target="tpu_custom_call" | custom-call | tf_op jit(solution)/shard_map/block/pallas_call | solution.py:548
  77.8 0.0 copy-start.3
  77.9 0.0 copy-done
  77.9 0.0 copy-done.4
  77.9 0.7 copy-done.3
  78.5 0.0 copy-start.1
  78.5 1.1 %copy-done.1 = bf16[192,8,256]{2,1,0:T(8,128)(2,1)S(1)} copy-done((bf16[192,8,256]{2,1,0:T(8,128)(2,1)S(1)}, bf16[192,8,256]{2,1,0:T(8,128)(2,1)}, u32[]{:S(2)}) %copy-start.1) | copy-done | bytes 786456
  79.7 0.0 copy-start.2
  79.7 1.0 %copy-done.2 = bf16[2,16,48,128]{3,2,1,0:T(8,128)(2,1)S(1)} copy-done((bf16[2,16,48,128]{3,2,1,0:T(8,128)(2,1)S(1)}, bf16[2,16,48,128]{3,2,1,0:T(8,128)(2,1)}, u32[]{:S(2)}) %copy-start.2) | copy-done | bytes 393240
  80.7 1.8 %finish.1 = (bf16[192,8,256]{2,1,0:T(8,128)(2,1)}, f32[192,576]{1,0:T(8,128)}, f32[3,3,576]{2,1,0:T(4,128)}, f32[192,192]{1,0:T(8,128)}, f32[1,4]{1,0:T(1,128)}, /*index=5*/f32[1,192]{1,0:T(1,128)}, f32[1,192]{1,0:T(1,128)}) custom-call(bf16[192,8,256]{2,1,0:T(8,128)(2,1)S(1)} %copy-done.1, bf16[2,16,48,128]{3,2,1,0:T(8,128)(2,1)S(1)} %copy-done.2, ...), custom_call_target="tpu_custom_call" | custom-call | tf_op jit(solution)/shard_map/finish/pallas_call | solution.py:602
Async XLA Ops:
  0.6 77.2 %copy-start = (bf16[576,192]{0,1:T(8,128)(2,1)S(1)}, bf16[576,192]{0,1:T(8,128)(2,1)}, u32[]{:S(2)}) copy-start(bf16[576,192]{0,1:T(8,128)(2,1)} %param.10) | copy-start | bytes 663556
  0.6 77.2 %copy-start.4 = (f32[192]{0:T(256)S(1)}, f32[192]{0:T(256)}, u32[]{:S(2)}) copy-start(f32[192]{0:T(256)} %param.15) | copy-start | bytes 2308
  77.8 0.7 copy-start.3
  78.5 1.1 %copy-start.1 = (bf16[192,8,256]{2,1,0:T(8,128)(2,1)S(1)}, bf16[192,8,256]{2,1,0:T(8,128)(2,1)}, u32[]{:S(2)}) copy-start(bf16[192,8,256]{2,1,0:T(8,128)(2,1)} %get-tuple-element.16.adjoint_ref) | copy-start | bytes 2359300
  79.7 1.0 %copy-start.2 = (bf16[2,16,48,128]{3,2,1,0:T(8,128)(2,1)S(1)}, bf16[2,16,48,128]{3,2,1,0:T(8,128)(2,1)}, u32[]{:S(2)}) copy-start(bf16[2,16,48,128]{3,2,1,0:T(8,128)(2,1)} %get-tuple-element.17.gath_ref) | copy-start | bytes 1179652

commit v5 on v4

--- a/solution.py
+++ b/solution.py
@@ -138,7 +138,7 @@
         normed = (standard * scale + offset).astype(BF16)
         return dot(mixer_ref[...], normed).astype(BF16)
 
-    @pl.loop(0, rows, unroll=2)
+    @pl.loop(0, rows, unroll=4)
     def _(r):
         standard, inverse = standardized(own_ref[r])
         std32[r] = standard
@@ -173,7 +173,7 @@
     lanes = lax.broadcasted_iota(jnp.int32, (group, width), 1)
 
     def mix(strips):
-        @pl.loop(0, 3 * channels // group)
+        @pl.loop(0, 3 * channels // group, unroll=2)
         def _(g):
             at = pl.ds(pl.multiple_of(g * group, group), group)
             weights = stencil_ref[at, :]
@@ -191,7 +191,7 @@
 
     acc[...] = jnp.zeros_like(acc)
 
-    @pl.loop(0, rows, unroll=2)
+    @pl.loop(0, rows, unroll=4)
     def _(r):
         q = mixed[r + 1, 0:channels, :]
         k = mixed[r + 1, channels : 2 * channels, :]
@@ -268,7 +268,7 @@
     extra[...] = jnp.zeros_like(extra)
     sacc[...] = jnp.zeros_like(sacc)
 
-    @pl.loop(0, rows, unroll=2)
+    @pl.loop(0, rows, unroll=4)
     def _(r):
         acc[2, :, 0:channels] += dot(cot_ref[r], mixed[r + 1, 2 * channels : 3 * channels, :], NT)
 
@@ -319,7 +319,7 @@
     qc = coef[:, 0:1]
     kc = coef[:, 1:2]
 
-    @pl.loop(0, rows + 2, unroll=2)
+    @pl.loop(0, rows + 2, unroll=5)
     def _(r):
         inside = jnp.logical_and(
             jnp.logical_or(r > 0, has_lo), jnp.logical_or(r < rows + 1, has_hi)
@@ -335,7 +335,7 @@
 
     lane_g = lax.broadcasted_iota(jnp.int32, (group, 128), 1)
 
-    @pl.loop(0, 3 * channels // group)
+    @pl.loop(0, 3 * channels // group, unroll=2)
     def _(g):
         at = pl.ds(pl.multiple_of(g * group, group), group)
         weights = stencil_ref[at, :]
@@ -350,7 +350,7 @@
             right = jnp.where(lanes == 0, 0.0, pltpu.roll(sums[2], 1, 1))
             gp[r, at, :] = (sums[1] + right + left).astype(BF16)
 
-    @pl.loop(0, 3 * channels // group)
+    @pl.loop(0, 3 * channels // group, unroll=2)
     def _(g):
         at = pl.ds(pl.multiple_of(g * group, group), group)
         tap = [jnp.zeros((group, 128), F32) for _ in range(9)]
@@ -369,7 +369,7 @@
             total = total + jnp.where(lane_g == 72 + t, s, 0.0)
         extra[at, :] = total
 
-    @pl.loop(0, rows, unroll=2)
+    @pl.loop(0, rows, unroll=4)
     def _(r):
         sacc[...] += dot(gp[r], ext[r], NT)
 
@@ -408,7 +408,7 @@
     others = pl.ds(0, groups - 1)
 
     def feature_rows(first_row, last_row):
-        @pl.loop(first_row, last_row, unroll=2)
+        @pl.loop(first_row, last_row, unroll=min(last_row - first_row, 4))
         def _(r):
             standard = std32[r]
             inverse = inv[r]
@@ -613,7 +613,7 @@
         in_specs=[anywhere] + [VMEM] * 4,
         out_specs=[anywhere] + [VMEM] * 6,
         scratch_shapes=[pltpu.SemaphoreType.DMA],
-        compiler_params=pltpu.CompilerParams(vmem_limit_bytes=32 * 1024 * 1024),
+        compiler_params=pltpu.CompilerParams(vmem_limit_bytes=LIMIT),
         name="finish",
     )(adjoint, gathered, mixer_t, scale_row, offset_row)
     return (

time: 82.7 us -> 97.3 us (1.18)
  Pallas kernels: 78.9 us -> 96.5 us
  local copies, waits for them, and re-layouts: 2.79 us -> 0 us
    pallas_call x1, Pallas kernels: 1.76 us -> 26.9 us  [local(): pl.pallas_call(finish_kernel, out_shape=(shape((channels, rows, width), B...]
    pallas_call x1, Pallas kernels: 77.2 us -> 69.6 us  [local(): pl.pallas_call(functools.partial(kernel, n_img, n_tile), out_shape=(shape...]
    unnamed x10 -> x0, local copies, waits for them, and re-layouts: 2.79 us -> none
where the time goes in v5:
time: 97.3 us; the launch traced here: 97.1 us
  Pallas kernels  96.5 us (99%)
    pallas_call x1, Pallas kernels, local(): pl.pallas_call(functools.partial(kernel, n_img, n_tile), out_shape=(shape...  69.6 us
    pallas_call x1, Pallas kernels, local(): pl.pallas_call(finish_kernel, out_shape=(shape((channels, rows, width), B...  26.9 us

profile of v5, /device:TPU:0, one launch (start us, length us, event | category | flops | bytes accessed | tf_op | source)
XLA Modules:
  0.0 97.1 jit_solution(13032699571038536060)
XLA Ops:
  0.6 69.6 %block.1 = (bf16[192,8,256]{2,1,0:T(8,128)(2,1)}, bf16[2,16,48,128]{3,2,1,0:T(8,128)(2,1)}) custom-call(bf16[192,8,256]{2,1,0:T(8,128)(2,1)} %bitcast.14, bf16[192,8,256]{2,1,0:T(8,128)(2,1)} %bitcast.15, bf16[192,576]{1,0:T(8,128)(2,1)} %bitcast.12, f32[3,3,576]{2,1,0:T(4,128)} %bitcast.16, bf16[192,192]{1,0:T(8,128)(2,1)} %out_mixer_ref.1, ...), custom_call_target="tpu_custom_call" | custom-call | tf_op jit(solution)/shard_map/block/pallas_call | solution.py:548
  70.2 26.9 %finish.1 = (bf16[192,8,256]{2,1,0:T(8,128)(2,1)}, f32[192,576]{1,0:T(8,128)}, f32[3,3,576]{2,1,0:T(4,128)}, f32[192,192]{1,0:T(8,128)}, f32[1,4]{1,0:T(1,128)}, /*index=5*/f32[1,192]{1,0:T(1,128)}, f32[1,192]{1,0:T(1,128)}) custom-call(bf16[192,8,256]{2,1,0:T(8,128)(2,1)} %get-tuple-element.16.adjoint_ref, ...), custom_call_target="tpu_custom_call" | custom-call | tf_op jit(solution)/shard_map/finish/pallas_call | solution.py:602

commit v6 on v4

--- a/solution.py
+++ b/solution.py
@@ -34,6 +34,21 @@
     return right, left
 
 
+def column_sums(w, line):
+    return [
+        jnp.concatenate(
+            [
+                w[b] * line[0][:, c : c + 128]
+                + w[3 + b] * line[1][:, c : c + 128]
+                + w[6 + b] * line[2][:, c : c + 128]
+                for c in range(0, line[0].shape[1], 128)
+            ],
+            axis=1,
+        )
+        for b in range(3)
+    ]
+
+
 def column(row):
     n = row.shape[1]
     eye = lax.broadcasted_iota(jnp.int32, (n, n), 0) == lax.broadcasted_iota(jnp.int32, (n, n), 1)
@@ -55,7 +70,7 @@
     n_img, n_tile,
     own_in, cot_in, mixer_t, stencil_in, out_mixer_ref, scale_ref, offset_ref, sharp_ref,
     out_ref, gath_out,
-    own32, cot32, std32, ext, inv, own_ref, cot_ref, mixer_ref, om_t, stencil_ref, lo, hi, proj, mixed, ga, gm, gp, acc, gram, gram_recv, gram_all, gg_ref, ggt_ref, at_ref, coef,
+    wide, own32, cot32, std32, ext, inv, own_ref, cot_ref, mixer_ref, om_t, stencil_ref, lo, hi, proj, mixed, ga, gm, gp, acc, gram, gram_recv, gram_all, gg_ref, ggt_ref, at_ref, coef,
     sacc, extra, red, pair, half, recv, gath,
     lo_x, lo_c, hi_x, hi_c, gram_rs, gram_ag, pair_rs, main_rs, pair_ag, ag_send, ag_recv,
 ):
@@ -130,23 +145,28 @@
         for copy in to_previous():
             copy.start()
 
-    scale = column(scale_ref[...])
-    offset = column(offset_ref[...])
+    wide[0] = jnp.broadcast_to(column(scale_ref[...]), (channels, 128))
+    wide[1] = jnp.broadcast_to(column(offset_ref[...]), (channels, 128))
+    halves = [slice(c, c + 128) for c in range(0, width, 128)]
 
     def project(x):
-        standard, _ = standardized(x)
-        normed = (standard * scale + offset).astype(BF16)
-        return dot(mixer_ref[...], normed).astype(BF16)
-
-    @pl.loop(0, rows, unroll=2)
+        parts = []
+        for c in halves:
+            standard, _ = standardized(x[:, c])
+            parts.append((standard * wide[0] + wide[1]).astype(BF16))
+        return dot(mixer_ref[...], jnp.concatenate(parts, axis=1)).astype(BF16)
+
+    @pl.loop(0, rows)
     def _(r):
-        standard, inverse = standardized(own_ref[r])
-        std32[r] = standard
-        inv[r] = inverse
-        ext[r, 0:channels, :] = standard.astype(BF16)
+        parts = []
+        for c in halves:
+            standard, inverse = standardized(own_ref[r, :, c])
+            std32[r, :, c] = standard
+            inv[r, :, c] = inverse
+            ext[r, 0:channels, c] = standard.astype(BF16)
+            parts.append((standard * wide[0] + wide[1]).astype(BF16))
         ext[r, channels:256, :] = jnp.ones((256 - channels, width), BF16)
-        normed = (standard * scale + offset).astype(BF16)
-        proj[r + 2] = dot(mixer_ref[...], normed).astype(BF16)
+        proj[r + 2] = dot(mixer_ref[...], jnp.concatenate(parts, axis=1)).astype(BF16)
         ga[r + 1] = dot(om_t[...], cot_ref[r]).astype(BF16)
 
     @pl.when(has_lo)
@@ -177,12 +197,12 @@
         def _(g):
             at = pl.ds(pl.multiple_of(g * group, group), group)
             weights = stencil_ref[at, :]
-            w = [jnp.broadcast_to(weights[:, t : t + 1], (group, width)) for t in range(9)]
+            w = [jnp.broadcast_to(weights[:, t : t + 1], (group, 128)) for t in range(9)]
             for first_row, last_row in strips:
                 line = [proj[first_row + i, at, :].astype(F32) for i in range(2)]
                 for r in range(first_row, last_row):
                     line = line[-2:] + [proj[r + 2, at, :].astype(F32)]
-                    sums = [w[b] * line[0] + w[3 + b] * line[1] + w[6 + b] * line[2] for b in range(3)]
+                    sums = column_sums(w, line)
                     right = jnp.where(lanes == 0, 0.0, pltpu.roll(sums[0], 1, 1))
                     left = jnp.where(lanes == width - 1, 0.0, pltpu.roll(sums[2], width - 1, 1))
                     mixed[r, at, :] = (sums[1] + right + left).astype(BF16)
@@ -191,7 +211,7 @@
 
     acc[...] = jnp.zeros_like(acc)
 
-    @pl.loop(0, rows, unroll=2)
+    @pl.loop(0, rows)
     def _(r):
         q = mixed[r + 1, 0:channels, :]
         k = mixed[r + 1, channels : 2 * channels, :]
@@ -268,7 +288,7 @@
     extra[...] = jnp.zeros_like(extra)
     sacc[...] = jnp.zeros_like(sacc)
 
-    @pl.loop(0, rows, unroll=2)
+    @pl.loop(0, rows)
     def _(r):
         acc[2, :, 0:channels] += dot(cot_ref[r], mixed[r + 1, 2 * channels : 3 * channels, :], NT)
 
@@ -316,21 +336,25 @@
 
     oma = dot(acc[2, :, 0:channels].astype(BF16), at_ref[...])
 
-    qc = coef[:, 0:1]
-    kc = coef[:, 1:2]
-
-    @pl.loop(0, rows + 2, unroll=2)
+    wide[2] = jnp.broadcast_to(coef[:, 0:1], (channels, 128))
+    wide[3] = jnp.broadcast_to(coef[:, 1:2], (channels, 128))
+
+    @pl.loop(0, rows + 2)
     def _(r):
         inside = jnp.logical_and(
             jnp.logical_or(r > 0, has_lo), jnp.logical_or(r < rows + 1, has_hi)
         ).astype(F32)
         q = mixed[r, 0:channels, :]
         k = mixed[r, channels : 2 * channels, :]
-        gq = dot(gg_ref[...], k) - q.astype(F32) * qc
-        gk = dot(ggt_ref[...], q) - k.astype(F32) * kc
+        gq = dot(gg_ref[...], k)
+        for c in halves:
+            gm[r, 0:channels, c] = ((gq[:, c] - q[:, c].astype(F32) * wide[2]) * inside).astype(BF16)
+        gk = dot(ggt_ref[...], q)
+        for c in halves:
+            gm[r, channels : 2 * channels, c] = (
+                (gk[:, c] - k[:, c].astype(F32) * wide[3]) * inside
+            ).astype(BF16)
         gv = dot(at_ref[...], ga[r])
-        gm[r, 0:channels, :] = (gq * inside).astype(BF16)
-        gm[r, channels : 2 * channels, :] = (gk * inside).astype(BF16)
         gm[r, 2 * channels : 3 * channels, :] = (gv * inside).astype(BF16)
 
     lane_g = lax.broadcasted_iota(jnp.int32, (group, 128), 1)
@@ -339,13 +363,11 @@
     def _(g):
         at = pl.ds(pl.multiple_of(g * group, group), group)
         weights = stencil_ref[at, :]
-        w = [jnp.broadcast_to(weights[:, t : t + 1], (group, width)) for t in range(9)]
+        w = [jnp.broadcast_to(weights[:, t : t + 1], (group, 128)) for t in range(9)]
         line = [gm[i, at, :].astype(F32) for i in range(2)]
         for r in range(rows):
             line.append(gm[r + 2, at, :].astype(F32))
-            sums = [
-                w[b] * line[r + 2] + w[3 + b] * line[r + 1] + w[6 + b] * line[r] for b in range(3)
-            ]
+            sums = column_sums(w, line[r : r + 3][::-1])
             left = jnp.where(lanes == width - 1, 0.0, pltpu.roll(sums[0], width - 1, 1))
             right = jnp.where(lanes == 0, 0.0, pltpu.roll(sums[2], 1, 1))
             gp[r, at, :] = (sums[1] + right + left).astype(BF16)
@@ -369,7 +391,7 @@
             total = total + jnp.where(lane_g == 72 + t, s, 0.0)
         extra[at, :] = total
 
-    @pl.loop(0, rows, unroll=2)
+    @pl.loop(0, rows)
     def _(r):
         sacc[...] += dot(gp[r], ext[r], NT)
 
@@ -408,18 +430,17 @@
     others = pl.ds(0, groups - 1)
 
     def feature_rows(first_row, last_row):
-        @pl.loop(first_row, last_row, unroll=2)
+        @pl.loop(first_row, last_row)
         def _(r):
-            standard = std32[r]
-            inverse = inv[r]
-            scaled = dot(mixer_t[...], gp[r]) * scale
-            first = jnp.mean(scaled, axis=0, keepdims=True)
-            second = jnp.mean(scaled * standard, axis=0, keepdims=True)
-            adjoint = cot_ref[r].astype(F32) + (scaled - first - standard * second) * inverse
-            for c in range(width // 128):
-                own32[pl.ds(c * channels * rows + r, channels, stride=rows), :] = adjoint[
-                    :, 128 * c : 128 * c + 128
-                ]
+            grad_normed = dot(mixer_t[...], gp[r])
+            for i, c in enumerate(halves):
+                standard = std32[r, :, c]
+                scaled = grad_normed[:, c] * wide[0]
+                first = jnp.mean(scaled, axis=0, keepdims=True)
+                second = jnp.mean(scaled * standard, axis=0, keepdims=True)
+                own32[pl.ds(i * channels * rows + r, channels, stride=rows), :] = cot_ref[
+                    r, :, c
+                ].astype(F32) + (scaled - first - standard * second) * inv[r, :, c]
 
     swap = remote(red.at[1 - core], pair, pair_rs, partner)
     swap.start()
@@ -554,6 +575,7 @@
         in_specs=[VMEM] * 7 + [SMEM],
         out_specs=[VMEM] * 2,
         scratch_shapes=[
+            vmem((4, channels, 128), F32),
             vmem((channels * rows * width // 128, 128), F32),
             vmem((channels * rows * width // 128, 128), F32),
             vmem((rows, channels, width), F32),
@@ -613,7 +635,7 @@
         in_specs=[anywhere] + [VMEM] * 4,
         out_specs=[anywhere] + [VMEM] * 6,
         scratch_shapes=[pltpu.SemaphoreType.DMA],
-        compiler_params=pltpu.CompilerParams(vmem_limit_bytes=32 * 1024 * 1024),
+        compiler_params=pltpu.CompilerParams(vmem_limit_bytes=LIMIT),
         name="finish",
     )(adjoint, gathered, mixer_t, scale_row, offset_row)
     return (

time: 82.7 us -> 107 us (1.29)
  Pallas kernels: 78.9 us -> 106 us
  local copies, waits for them, and re-layouts: 2.79 us -> 0 us
    pallas_call x1, Pallas kernels: 1.76 us -> 26.9 us  [local(): pl.pallas_call(finish_kernel, out_shape=(shape((channels, rows, width), B...]
    unnamed x10 -> x0, local copies, waits for them, and re-layouts: 2.79 us -> none
    pallas_call x1, Pallas kernels: 77.2 us -> 79.5 us  [local(): pl.pallas_call(functools.partial(kernel, n_img, n_tile), out_shape=(shape...]
where the time goes in v6:
time: 107 us
  Pallas kernels  106 us (99%)
    pallas_call x1, Pallas kernels, local(): pl.pallas_call(functools.partial(kernel, n_img, n_tile), out_shape=(shape...  79.5 us
    pallas_call x1, Pallas kernels, local(): pl.pallas_call(finish_kernel, out_shape=(shape((channels, rows, width), B...  26.9 us

profile of v6, /device:TPU:0, one launch (start us, length us, event | category | flops | bytes accessed | tf_op | source)
XLA Modules:
  0.0 107.0 jit_solution(2985173813698008781)
XLA Ops:
  0.6 79.5 %block.1 = (bf16[192,8,256]{2,1,0:T(8,128)(2,1)}, bf16[2,16,48,128]{3,2,1,0:T(8,128)(2,1)}) custom-call(bf16[192,8,256]{2,1,0:T(8,128)(2,1)} %bitcast.14, bf16[192,8,256]{2,1,0:T(8,128)(2,1)} %bitcast.15, bf16[192,576]{1,0:T(8,128)(2,1)} %bitcast.12, f32[3,3,576]{2,1,0:T(4,128)} %bitcast.16, bf16[192,192]{1,0:T(8,128)(2,1)} %out_mixer_ref.1, ...), custom_call_target="tpu_custom_call" | custom-call | tf_op jit(solution)/shard_map/block/pallas_call | solution.py:569
  80.1 26.9 %finish.1 = (bf16[192,8,256]{2,1,0:T(8,128)(2,1)}, f32[192,576]{1,0:T(8,128)}, f32[3,3,576]{2,1,0:T(4,128)}, f32[192,192]{1,0:T(8,128)}, f32[1,4]{1,0:T(1,128)}, /*index=5*/f32[1,192]{1,0:T(1,128)}, f32[1,192]{1,0:T(1,128)}) custom-call(bf16[192,8,256]{2,1,0:T(8,128)(2,1)} %get-tuple-element.16.adjoint_ref, ...), custom_call_target="tpu_custom_call" | custom-call | tf_op jit(solution)/shard_map/finish/pallas_call | solution.py:624
